TPU v7x, 32 devices: a whole 2x2x4 slice. The times are simulated.
32 devices in a mesh: dev: 32 (over z, y, x, core).
Axes of the slice: x: 2, y: 2, z: 4, core: 2. Of those that a mesh axis runs over, the one named last changes fastest.
Arguments:
- tokens: bfloat16 [8192, 192], P('dev'), may hold values from -6 to 6
- ranges: int32 [32, 2], replicated, may hold values from 0 to 7936, as said below
- attn_in: bfloat16 [2, 110592], P(None, 'dev'), may hold values from -0.4375 to 0.4375
- attn_out: bfloat16 [2, 36864], P(None, 'dev'), may hold values from -3.5 to 3.5
- mlp_in: bfloat16 [2, 147456], P(None, 'dev'), may hold values from -0.4375 to 0.4375
- mlp_out: bfloat16 [2, 147456], P(None, 'dev'), may hold values from -0.21875 to 0.21875
- vectors: bfloat16 [2, 2304], P(None, 'dev'), may hold values from -0.75 to 1.5, as said below
- cotangent: bfloat16 [8192, 192], P('dev'), may hold values from -6 to 6
Outputs:
- activations: bfloat16 [8192, 192], P('dev')
- input_grad: float32 [8192, 192], P('dev')
- attn_in_grad: float32 [2, 110592], P(None, 'dev')
- attn_out_grad: float32 [2, 36864], P(None, 'dev')
- mlp_in_grad: float32 [2, 147456], P(None, 'dev')
- mlp_out_grad: float32 [2, 147456], P(None, 'dev')
- vectors_grad: float32 [2, 2304], P(None, 'dev')
Inputs may be any that keep to these rules, and one draw needn't show every extreme that they name: Row j gives the range of stream positions on device j; ranges follow one another from 0 to 7936; each device holds 240 to 256 tokens, some device exactly 256. `vectors`: norm gains lie within 0.5 to 1.5.
All inputs are finite; a program needn't handle non-finite values.
Results may differ from a plain program's by a relative error of at most 0.01.
Values may be sent and summed in bfloat16 or wider, within the bound.
A program may use at most 64 MiB of HBM per device.

v0:
```python
import math

import jax
import jax.numpy as jnp
from jax import lax
from jax.sharding import PartitionSpec as P

HD = 64
IMG_LEN = 197


eps_norm = 1e-06
masked_fill = -1e30


def shortened(array):

    def short(part):
        return part.astype(jnp.bfloat16) if part.dtype == jnp.float32 else part

    return jax.tree.map(short, array)


def shifted(array, axis, by):
    size = lax.axis_size(axis)
    pairs = [(i, i + by) for i in range(size) if 0 <= i + by < size]
    return lax.ppermute(array, axis, pairs)


def norm_forward(hidden, gain_vec, bias_vec):
    row_mean = jnp.mean(hidden, axis=-1, keepdims=True)
    centered = hidden - row_mean
    variance = jnp.mean(centered * centered, axis=-1, keepdims=True)
    inverse = lax.rsqrt(variance + eps_norm)
    normal_hat = centered * inverse
    return (normal_hat * gain_vec + bias_vec, normal_hat, inverse)


def norm_backward(grad_out, normal_hat, inverse, gain_vec):
    scaled = grad_out * gain_vec
    grad_in = inverse * (
        scaled
        - jnp.mean(scaled, axis=-1, keepdims=True)
        - normal_hat * jnp.mean(scaled * normal_hat, axis=-1, keepdims=True)
    )
    return (grad_in, jnp.sum(grad_out * normal_hat, axis=0), jnp.sum(grad_out, axis=0))


def gelu_slope(pre_gelu):
    cumulative = 0.5 * (1.0 + lax.erf(pre_gelu * (1.0 / math.sqrt(2.0))))
    density = jnp.exp(-0.5 * pre_gelu * pre_gelu) * (1.0 / math.sqrt(2.0 * math.pi))
    return cumulative + pre_gelu * density


def neighbour_images(ranges, offset, own_index, device_count, slot_count, empty_id):
    dev_index = own_index + offset
    present = (dev_index >= 0) & (dev_index < device_count)
    clipped = jnp.clip(dev_index, 0, device_count - 1)
    start_pos = ranges[clipped, 0]
    length = jnp.where(present, ranges[clipped, 1] - start_pos, 0)
    slot_ids = jnp.arange(slot_count, dtype=jnp.int32)
    return jnp.where(slot_ids < length, (start_pos + slot_ids) // IMG_LEN, empty_id)


def unpack(gathered, model_width):
    w_in_flat, w_out_flat, w_one_flat, w_two_flat, vector_flat = gathered
    hidden_units = w_one_flat.shape[0] // model_width
    vector_all = vector_flat.astype(jnp.float32)
    pieces = tuple(
        (
            vector_all[piece_index * model_width : (piece_index + 1) * model_width]
            for piece_index in range(8)
        )
    )
    return (
        (
            w_in_flat.reshape(model_width, 3 * model_width),
            w_out_flat.reshape(model_width, model_width),
            w_one_flat.reshape(model_width, hidden_units),
            w_two_flat.reshape(hidden_units, model_width),
        )
        + pieces
        + (vector_all[8 * model_width :],)
    )


def from_lower(payload):
    return jax.tree.map(
        lambda part, own: part.astype(own.dtype), shifted(shortened(payload), "dev", 1), payload
    )


def from_upper(payload):
    return jax.tree.map(
        lambda part, own: part.astype(own.dtype), shifted(shortened(payload), "dev", -1), payload
    )


def back_down(payload):
    return shifted((shortened(payload[0]), shortened(payload[1])), "dev", -1)


def back_up(payload):
    return shifted((shortened(payload[0]), shortened(payload[1])), "dev", 1)


def score_block(queries, key_rows, same_image, score_scale):
    scores = (
        jnp.einsum("qhd,khd->hqk", queries, key_rows, preferred_element_type=jnp.float32)
        * score_scale
    )
    return jnp.where(same_image[None, :, :], scores, masked_fill)


def layer_forward(hidden, params, same_image, head_count, score_scale):
    (
        w_in,
        w_out,
        w_one,
        w_two,
        ln1_gain,
        ln1_bias,
        q_bias,
        v_bias,
        out_bias,
        ln2_gain,
        ln2_bias,
        two_bias,
        one_bias,
    ) = params
    slot_count, model_width = hidden.shape
    head_size = model_width // head_count
    normed, hat_one, inv_one = norm_forward(hidden, ln1_gain, ln1_bias)
    normed_low = normed.astype(jnp.bfloat16)
    projected = jnp.dot(normed_low, w_in, preferred_element_type=jnp.float32)
    queries = (projected[:, 0:model_width] + q_bias).astype(jnp.bfloat16)
    key_rows = projected[:, model_width : 2 * model_width].astype(jnp.bfloat16)
    values = (projected[:, 2 * model_width :] + v_bias).astype(jnp.bfloat16)
    lower_one = from_lower((key_rows, values))
    lower_two = from_lower(lower_one)
    upper_one = from_upper((key_rows, values))
    upper_two = from_upper(upper_one)
    all_keys = jnp.concatenate(
        [lower_two[0], lower_one[0], key_rows, upper_one[0], upper_two[0]], axis=0
    )
    all_values = jnp.concatenate(
        [lower_two[1], lower_one[1], values, upper_one[1], upper_two[1]], axis=0
    )
    all_keys = all_keys.reshape(5 * slot_count, head_count, head_size)
    all_values = all_values.reshape(5 * slot_count, head_count, head_size)
    head_queries = queries.reshape(slot_count, head_count, head_size)
    scores = score_block(head_queries, all_keys, same_image, score_scale)
    row_max = jnp.max(scores, axis=-1, keepdims=True)
    exponent = jnp.exp(scores - row_max)
    row_total = jnp.sum(exponent, axis=-1, keepdims=True)
    softmax_weights = exponent / row_total
    log_total = row_max + jnp.log(row_total)
    context = jnp.einsum(
        "hqk,khd->qhd",
        softmax_weights.astype(jnp.bfloat16),
        all_values,
        preferred_element_type=jnp.float32,
    )
    context = context.reshape(slot_count, model_width).astype(jnp.bfloat16)
    mid_stream = hidden + (jnp.dot(context, w_out, preferred_element_type=jnp.float32) + out_bias)
    normed_two, hat_two, inv_two = norm_forward(mid_stream, ln2_gain, ln2_bias)
    normed_two_low = normed_two.astype(jnp.bfloat16)
    pre_gelu = jnp.dot(normed_two_low, w_one, preferred_element_type=jnp.float32) + one_bias
    activation = jax.nn.gelu(pre_gelu, approximate=False).astype(jnp.bfloat16)
    result = mid_stream + (
        jnp.dot(activation, w_two, preferred_element_type=jnp.float32) + two_bias
    )
    record = (
        hat_one,
        inv_one,
        normed_low,
        head_queries,
        all_keys,
        all_values,
        log_total,
        context,
        hat_two,
        inv_two,
        normed_two_low,
        pre_gelu,
        activation,
    )
    return (result, record)


def column_sum(rows_low):
    return jnp.sum(rows_low.astype(jnp.float32), axis=0)


def layer_backward(upstream, params, record, same_image, score_scale):
    (
        w_in,
        w_out,
        w_one,
        w_two,
        ln1_gain,
        ln1_bias,
        q_bias,
        v_bias,
        out_bias,
        ln2_gain,
        ln2_bias,
        two_bias,
        one_bias,
    ) = params
    (
        hat_one,
        inv_one,
        normed_low,
        head_queries,
        all_keys,
        all_values,
        log_total,
        context,
        hat_two,
        inv_two,
        normed_two_low,
        pre_gelu,
        activation,
    ) = record
    slot_count, model_width = upstream.shape
    grad_mlp = upstream.astype(jnp.bfloat16)
    two_bias_grad = column_sum(grad_mlp)
    w_two_grad = jnp.einsum("tf,td->fd", activation, grad_mlp, preferred_element_type=jnp.float32)
    grad_activ = jnp.einsum("td,fd->tf", grad_mlp, w_two, preferred_element_type=jnp.float32)
    grad_pre = (grad_activ * gelu_slope(pre_gelu)).astype(jnp.bfloat16)
    one_bias_grad = column_sum(grad_pre)
    w_one_grad = jnp.einsum(
        "td,tf->df", normed_two_low, grad_pre, preferred_element_type=jnp.float32
    )
    grad_normed_two = jnp.einsum("tf,df->td", grad_pre, w_one, preferred_element_type=jnp.float32)
    grad_ln_two, ln2_gain_grad, ln2_bias_grad = norm_backward(
        grad_normed_two, hat_two, inv_two, ln2_gain
    )
    grad_mid = upstream + grad_ln_two
    grad_branch = grad_mid.astype(jnp.bfloat16)
    out_bias_grad = column_sum(grad_branch)
    w_out_grad = jnp.einsum("tc,td->cd", context, grad_branch, preferred_element_type=jnp.float32)
    grad_context = jnp.einsum("td,cd->tc", grad_branch, w_out, preferred_element_type=jnp.float32)
    grad_context = grad_context.astype(jnp.bfloat16).reshape(head_queries.shape)
    scores = score_block(head_queries, all_keys, same_image, score_scale)
    softmax_weights = jnp.exp(scores - log_total)
    grad_weights = jnp.einsum(
        "qhd,khd->hqk", grad_context, all_values, preferred_element_type=jnp.float32
    )
    delta = jnp.sum(softmax_weights * grad_weights, axis=-1, keepdims=True)
    grad_scores = (softmax_weights * (grad_weights - delta)).astype(jnp.bfloat16)
    grad_queries = (
        jnp.einsum("hqk,khd->qhd", grad_scores, all_keys, preferred_element_type=jnp.float32)
        * score_scale
    )
    grad_keys_all = (
        jnp.einsum("hqk,qhd->khd", grad_scores, head_queries, preferred_element_type=jnp.float32)
        * score_scale
    )
    grad_values_all = jnp.einsum(
        "hqk,qhd->khd",
        softmax_weights.astype(jnp.bfloat16),
        grad_context,
        preferred_element_type=jnp.float32,
    )
    grad_keys_all = grad_keys_all.reshape(5, slot_count, model_width)
    grad_values_all = grad_values_all.reshape(5, slot_count, model_width)
    down_one = back_down((grad_keys_all[0], grad_values_all[0]))
    down_two = back_down((grad_keys_all[1] + down_one[0], grad_values_all[1] + down_one[1]))
    up_one = back_up((grad_keys_all[4], grad_values_all[4]))
    up_two = back_up((grad_keys_all[3] + up_one[0], grad_values_all[3] + up_one[1]))
    key_grad = (grad_keys_all[2] + down_two[0] + up_two[0]).astype(jnp.bfloat16)
    value_grad = (grad_values_all[2] + down_two[1] + up_two[1]).astype(jnp.bfloat16)
    query_grad = grad_queries.reshape(slot_count, model_width).astype(jnp.bfloat16)
    q_bias_grad = column_sum(query_grad)
    v_bias_grad = column_sum(value_grad)
    grad_projected = jnp.concatenate([query_grad, key_grad, value_grad], axis=1)
    w_in_grad = jnp.einsum(
        "td,tc->dc", normed_low, grad_projected, preferred_element_type=jnp.float32
    )
    grad_normed = jnp.einsum("tc,dc->td", grad_projected, w_in, preferred_element_type=jnp.float32)
    grad_ln_one, ln1_gain_grad, ln1_bias_grad = norm_backward(
        grad_normed, hat_one, inv_one, ln1_gain
    )
    grad_input = grad_mid + grad_ln_one
    vector_grad = jnp.concatenate(
        [
            ln1_gain_grad,
            ln1_bias_grad,
            q_bias_grad,
            v_bias_grad,
            out_bias_grad,
            ln2_gain_grad,
            ln2_bias_grad,
            two_bias_grad,
            one_bias_grad,
        ],
        axis=0,
    )
    grad_terms = (
        w_in_grad.reshape(-1),
        w_out_grad.reshape(-1),
        w_one_grad.reshape(-1),
        w_two_grad.reshape(-1),
        vector_grad,
    )
    return (grad_input, grad_terms)


def local(tokens, ranges, attn_in, attn_out, mlp_in, mlp_out, vectors, cotangent):
    device_count = lax.axis_size("dev")
    own_index = lax.axis_index("dev")
    slot_count, model_width = tokens.shape
    head_count = model_width // HD
    score_scale = 1.0 / math.sqrt(HD)
    layer_total = attn_in.shape[0]
    own_ids = neighbour_images(ranges, 0, own_index, device_count, slot_count, -1)
    is_token = own_ids >= 0
    key_ids = jnp.concatenate(
        [
            neighbour_images(ranges, offset, own_index, device_count, slot_count, -2)
            for offset in (-2, -1, 0, 1, 2)
        ],
        axis=0,
    )
    same_image = own_ids[:, None] == key_ids[None, :]
    hidden = tokens.astype(jnp.float32)
    stored = []
    for layer_index in range(layer_total):
        gathered = (
            lax.all_gather(attn_in[layer_index], "dev", axis=0, tiled=True),
            lax.all_gather(attn_out[layer_index], "dev", axis=0, tiled=True),
            lax.all_gather(mlp_in[layer_index], "dev", axis=0, tiled=True),
            lax.all_gather(mlp_out[layer_index], "dev", axis=0, tiled=True),
            lax.all_gather(vectors[layer_index], "dev", axis=0, tiled=True),
        )
        params = unpack(gathered, model_width)
        hidden, record = layer_forward(hidden, params, same_image, head_count, score_scale)
        stored.append((params, record))
    activations = jnp.where(is_token[:, None], hidden, 0.0).astype(jnp.bfloat16)
    upstream = jnp.where(is_token[:, None], cotangent.astype(jnp.float32), 0.0)
    summed = [None] * layer_total
    for layer_index in reversed(range(layer_total)):
        params, record = stored[layer_index]
        regathered = (
            lax.all_gather(attn_in[layer_index], "dev", axis=0, tiled=True),
            lax.all_gather(attn_out[layer_index], "dev", axis=0, tiled=True),
            lax.all_gather(mlp_in[layer_index], "dev", axis=0, tiled=True),
            lax.all_gather(mlp_out[layer_index], "dev", axis=0, tiled=True),
            lax.all_gather(vectors[layer_index], "dev", axis=0, tiled=True),
        )
        params = unpack(regathered, model_width)
        upstream, grad_terms = layer_backward(upstream, params, record, same_image, score_scale)
        summed[layer_index] = (
            lax.psum_scatter(grad_terms[0], "dev", scatter_dimension=0, tiled=True),
            lax.psum_scatter(grad_terms[1], "dev", scatter_dimension=0, tiled=True),
            lax.psum_scatter(grad_terms[2], "dev", scatter_dimension=0, tiled=True),
            lax.psum_scatter(grad_terms[3], "dev", scatter_dimension=0, tiled=True),
            lax.psum_scatter(grad_terms[4], "dev", scatter_dimension=0, tiled=True),
        )
    input_grad = jnp.where(is_token[:, None], upstream, 0.0)
    attn_in_grad = jnp.stack([summed[layer_index][0] for layer_index in range(layer_total)], axis=0)
    attn_out_grad = jnp.stack(
        [summed[layer_index][1] for layer_index in range(layer_total)], axis=0
    )
    mlp_in_grad = jnp.stack([summed[layer_index][2] for layer_index in range(layer_total)], axis=0)
    mlp_out_grad = jnp.stack([summed[layer_index][3] for layer_index in range(layer_total)], axis=0)
    vectors_grad = jnp.stack([summed[layer_index][4] for layer_index in range(layer_total)], axis=0)
    return (
        activations,
        input_grad,
        attn_in_grad,
        attn_out_grad,
        mlp_in_grad,
        mlp_out_grad,
        vectors_grad,
    )


def solution(mesh):
    return jax.shard_map(
        local,
        mesh=mesh,
        in_specs=(
            P("dev", None),
            P(),
            P(None, "dev"),
            P(None, "dev"),
            P(None, "dev"),
            P(None, "dev"),
            P(None, "dev"),
            P("dev", None),
        ),
        out_specs=(
            P("dev", None),
            P("dev", None),
            P(None, "dev"),
            P(None, "dev"),
            P(None, "dev"),
            P(None, "dev"),
            P(None, "dev"),
        ),
        check_vma=False,
    )
```

profile of v0, /device:TPU:0, one launch (start us, length us, event | category | flops | bytes accessed | tf_op | source)
XLA Modules:
  0.0 752.4 jit_solution(16493871743259619341)
XLA Ops:
  8.4 42.2 %all-reduce.14 = (bf16[2304]{0:T(1024)(128)(2,1)S(1)}, bf16[2304]{0:T(1024)(128)(2,1)S(1)}) all-reduce(bf16[2304]{0:T(1024)(128)(2,1)S(1)} %dynamic-update-slice, bf16[2304]{0:T(1024)(128)(2,1)S(1)} %dynamic-update-slice.1), channel_id=2, replica_groups=mesh['dev'=32] {'dev'}, use_global_device_ids=true, to_apply=%add | all-reduce | flops 4608 | bytes 18432
  51.5 41.5 %all-gather.1 = bf16[1,110592]{1,0:T(2,128)(2,1)S(1)} all-gather(bf16[1,3456]{1,0:T(2,128)(2,1)S(1)} %get-tuple-element.71), channel_id=3, replica_groups=mesh['dev'=32] {'dev'}, dimensions={1}, use_global_device_ids=true | all-gather | bytes 228096 | tf_op jit(solution)/shard_map/all_gather | solution.py:332
  107.9 39.6 %all-gather.2 = bf16[1,36864]{1,0:T(2,128)(2,1)S(1)} all-gather(bf16[1,1152]{1,0:T(2,128)(2,1)S(1)} %get-tuple-element.89), channel_id=4, replica_groups=mesh['dev'=32] {'dev'}, dimensions={1}, use_global_device_ids=true | all-gather | bytes 76032 | tf_op jit(solution)/shard_map/all_gather | solution.py:333
  148.7 38.2 %all-gather.3 = bf16[1,147456]{1,0:T(2,128)(2,1)S(1)} all-gather(bf16[1,4608]{1,0:T(2,128)(2,1)S(1)} %get-tuple-element.69), channel_id=5, replica_groups=mesh['dev'=32] {'dev'}, dimensions={1}, use_global_device_ids=true | all-gather | bytes 304128 | tf_op jit(solution)/shard_map/all_gather | solution.py:334
  187.0 6.1 reduce.6
  193.4 40.2 %all-gather.4 = bf16[1,147456]{1,0:T(2,128)(2,1)S(1)} all-gather(bf16[1,4608]{1,0:T(2,128)(2,1)S(1)} %get-tuple-element.67), channel_id=6, replica_groups=mesh['dev'=32] {'dev'}, dimensions={1}, use_global_device_ids=true | all-gather | bytes 304128 | tf_op jit(solution)/shard_map/all_gather | solution.py:335
  233.7 6.1 reduce.8
  240.8 37.8 %all-gather.6 = bf16[1,110592]{1,0:T(2,128)(2,1)S(1)} all-gather(bf16[1,3456]{1,0:T(2,128)(2,1)S(1)} %get-tuple-element.70), channel_id=8, replica_groups=mesh['dev'=32] {'dev'}, dimensions={1}, use_global_device_ids=true | all-gather | bytes 228096 | tf_op jit(solution)/shard_map/all_gather | solution.py:332
  280.1 38.4 %all-gather.7 = bf16[1,36864]{1,0:T(2,128)(2,1)S(1)} all-gather(bf16[1,1152]{1,0:T(2,128)(2,1)S(1)} %get-tuple-element.88), channel_id=9, replica_groups=mesh['dev'=32] {'dev'}, dimensions={1}, use_global_device_ids=true | all-gather | bytes 76032 | tf_op jit(solution)/shard_map/all_gather | solution.py:333
  319.7 38.2 %all-gather.8 = bf16[1,147456]{1,0:T(2,128)(2,1)S(1)} all-gather(bf16[1,4608]{1,0:T(2,128)(2,1)S(1)} %get-tuple-element.68), channel_id=10, replica_groups=mesh['dev'=32] {'dev'}, dimensions={1}, use_global_device_ids=true | all-gather | bytes 304128 | tf_op jit(solution)/shard_map/all_gather | solution.py:334
  357.9 6.1 reduce.11
  364.3 39.9 %all-gather.9 = bf16[1,147456]{1,0:T(2,128)(2,1)S(1)} all-gather(bf16[1,4608]{1,0:T(2,128)(2,1)S(1)} %get-tuple-element.66), channel_id=11, replica_groups=mesh['dev'=32] {'dev'}, dimensions={1}, use_global_device_ids=true | all-gather | bytes 304128 | tf_op jit(solution)/shard_map/all_gather | solution.py:335
  404.2 6.1 reduce.13
  440.8 5.1 collective-permute-start.8
  452.3 4.2 collective-permute-start.9
  457.8 4.3 collective-permute-start.13
  482.6 7.2 collective-permute-start.22
  502.8 5.0 collective-permute-start.23
  511.2 4.3 collective-permute-start.19
  537.8 5.9 collective-permute-start.30
  558.1 6.1 collective-permute-start.31
  567.3 4.3 collective-permute-start.27
  581.5 54.2 %all-reduce.12 = (f32[2304]{0:T(1024)S(1)}, f32[2304]{0:T(1024)S(1)}) all-reduce(f32[2304]{0:T(1024)S(1)} %concatenate.35, f32[2304]{0:T(1024)S(1)} %concatenate.34), channel_id=21, replica_groups=mesh['dev'=32] {'dev'}, use_global_device_ids=true, to_apply=%region_49.50.clone | all-reduce | flops 4608 | bytes 36864
  637.2 98.8 %all-reduce.17.cloned.1.call-done = (f32[110592]{0:T(1024)}, f32[110592]{0:T(1024)}, f32[36864]{0:T(1024)}, f32[36864]{0:T(1024)}, f32[147456]{0:T(1024)}, /*ind...) async-done(((f32[110592]{0:T(1024)}, f32[110592]{0:T(1024)}, f32[36864]{0:T(1024)}, f32[36864]{0:T(1024)}, f32[147456]{0:T(1024)}, /*index=5*/f32[147456]{0:T(1024)}, ...) | async-done | bytes 3538960
  (377 shorter events, 150.2 us)
Async XLA Ops:
  7.2 728.8 %all-reduce.17.cloned.1.call-start = ((), (), s32[]{:S(2)}) async-start(), calls=%async_computation | async-start | bytes 7077888
  98.0 323.8 %collective-permute-start = (bf16[256,192]{0,1:T(8,128)(2,1)S(1)}, bf16[256,192]{0,1:T(8,128)(2,1)}, u32[]{:S(2)}, u32[]{:S(2)}) collective-permute-start(bf16[256,192]{0,1:T(8,128)(2,1)S(1)} %get-tuple-element.56), channel_id=1, source_target_pairs={{0,1},{1,2},{2,3},{3,4},{4,5},{5,6},{6,7},{7,8},{8,9},{9,10},{10,1... | collective-permute-start | bytes 294920 | tf_op jit(solution)/shard_map/ppermute | solution.py:27
  100.9 323.2 %collective-permute-start.2 = (bf16[256,192]{0,1:T(8,128)(2,1)S(1)}, bf16[256,192]{0,1:T(8,128)(2,1)}, u32[]{:S(2)}, u32[]{:S(2)}) collective-permute-start(bf16[256,192]{0,1:T(8,128)(2,1)S(1)} %get-tuple-element.56), channel_id=1, source_target_pairs={{1,0},{2,1},{3,2},{4,3},{5,4},{6,5},{7,6},{8,7},{9,8},{10,9},{11,1... | collective-permute-start | bytes 294920 | tf_op jit(solution)/shard_map/ppermute | solution.py:27
  102.8 322.5 %collective-permute-start.4 = (bf16[256,192]{0,1:T(8,128)(2,1)}, bf16[256,192]{0,1:T(8,128)(2,1)S(1)}, u32[]{:S(2)}, u32[]{:S(2)}) collective-permute-start(bf16[256,192]{0,1:T(8,128)(2,1)} %slice.341), channel_id=1, source_target_pairs={{0,1},{1,2},{2,3},{3,4},{4,5},{5,6},{6,7},{7,8},{8,9},{9,10},{10,1... | collective-permute-start | bytes 294920 | tf_op jit(solution)/shard_map/ppermute | solution.py:27
  105.8 322.6 %collective-permute-start.6 = (bf16[256,192]{0,1:T(8,128)(2,1)}, bf16[256,192]{0,1:T(8,128)(2,1)}, u32[]{:S(2)}, u32[]{:S(2)}) collective-permute-start(bf16[256,192]{0,1:T(8,128)(2,1)} %slice.341), channel_id=1, source_target_pairs={{1,0},{2,1},{3,2},{4,3},{5,4},{6,5},{7,6},{8,7},{9,8},{10,9},{11,1... | collective-permute-start | bytes 294920 | tf_op jit(solution)/shard_map/ppermute | solution.py:27
  424.0 11.4 %collective-permute-start.3 = (bf16[256,192]{0,1:T(8,128)(2,1)}, bf16[256,192]{0,1:T(8,128)(2,1)S(1)}, u32[]{:S(2)}, u32[]{:S(2)}) collective-permute-start(bf16[256,192]{0,1:T(8,128)(2,1)} %collective-permute-done.2), channel_id=1, source_target_pairs={{1,0},{2,1},{3,2},{4,3},{5,4},{6,5},{7,6},{8,7},{9,8},{10,9},{11,1... | collective-permute-start | bytes 294920 | tf_op jit(solution)/shard_map/ppermute | solution.py:27
  440.8 11.5 %collective-permute-start.8 = (bf16[256,192]{0,1:T(8,128)(2,1)S(1)}, bf16[256,192]{0,1:T(8,128)(2,1)S(1)}, u32[]{:S(2)}, u32[]{:S(2)}) collective-permute-start(bf16[256,192]{0,1:T(8,128)(2,1)S(1)} %get-tuple-element.54), channel_id=1, source_target_pairs={{0,1},{1,2},{2,3},{3,4},{4,5},{5,6},{6,7},{7,8},{8,9},{9,10},{10,1... | collective-permute-start | bytes 294920 | tf_op jit(solution)/shard_map/ppermute | solution.py:27
  446.6 9.9 %collective-permute-start.10 = (bf16[256,192]{0,1:T(8,128)(2,1)S(1)}, bf16[256,192]{0,1:T(8,128)(2,1)S(1)}, u32[]{:S(2)}, u32[]{:S(2)}) collective-permute-start(bf16[256,192]{0,1:T(8,128)(2,1)S(1)} %get-tuple-element.54), channel_id=1, source_target_pairs={{1,0},{2,1},{3,2},{4,3},{5,4},{6,5},{7,6},{8,7},{9,8},{10,9},{11,1... | collective-permute-start | bytes 294920 | tf_op jit(solution)/shard_map/ppermute | solution.py:27
  447.9 9.9 %collective-permute-start.12 = (bf16[256,192]{0,1:T(8,128)(2,1)S(1)}, bf16[256,192]{0,1:T(8,128)(2,1)S(1)}, u32[]{:S(2)}, u32[]{:S(2)}) collective-permute-start(bf16[256,192]{0,1:T(8,128)(2,1)S(1)} %slice.340), channel_id=1, source_target_pairs={{0,1},{1,2},{2,3},{3,4},{4,5},{5,6},{6,7},{7,8},{8,9},{9,10},{10,1... | collective-permute-start | bytes 294920 | tf_op jit(solution)/shard_map/ppermute | solution.py:27
  450.9 11.1 %collective-permute-start.14 = (bf16[256,192]{0,1:T(8,128)(2,1)S(1)}, bf16[256,192]{0,1:T(8,128)(2,1)S(1)}, u32[]{:S(2)}, u32[]{:S(2)}) collective-permute-start(bf16[256,192]{0,1:T(8,128)(2,1)S(1)} %slice.340), channel_id=1, source_target_pairs={{1,0},{2,1},{3,2},{4,3},{5,4},{6,5},{7,6},{8,7},{9,8},{10,9},{11,1... | collective-permute-start | bytes 294920 | tf_op jit(solution)/shard_map/ppermute | solution.py:27
  452.3 11.3 %collective-permute-start.9 = (bf16[256,192]{0,1:T(8,128)(2,1)S(1)}, bf16[256,192]{0,1:T(8,128)(2,1)S(1)}, u32[]{:S(2)}, u32[]{:S(2)}) collective-permute-start(bf16[256,192]{0,1:T(8,128)(2,1)S(1)} %collective-permute-done.8), channel_id=1, source_target_pairs={{0,1},{1,2},{2,3},{3,4},{4,5},{5,6},{6,7},{7,8},{8,9},{9,10},{10,1... | collective-permute-start | bytes 294920 | tf_op jit(solution)/shard_map/ppermute | solution.py:27
  456.5 11.9 %collective-permute-start.11 = (bf16[256,192]{0,1:T(8,128)(2,1)S(1)}, bf16[256,192]{0,1:T(8,128)(2,1)S(1)}, u32[]{:S(2)}, u32[]{:S(2)}) collective-permute-start(bf16[256,192]{0,1:T(8,128)(2,1)S(1)} %collective-permute-done.10), channel_id=1, source_target_pairs={{1,0},{2,1},{3,2},{4,3},{5,4},{6,5},{7,6},{8,7},{9,8},{10,9},{11,1... | collective-permute-start | bytes 294920 | tf_op jit(solution)/shard_map/ppermute | solution.py:27
  482.6 19.2 %collective-permute-start.22 = (bf16[256,192]{0,1:T(8,128)(2,1)}, bf16[256,192]{0,1:T(8,128)(2,1)}, u32[]{:S(2)}, u32[]{:S(2)}) collective-permute-start(bf16[256,192]{0,1:T(8,128)(2,1)} %bitcast.52), channel_id=1, source_target_pairs={{0,1},{1,2},{2,3},{3,4},{4,5},{5,6},{6,7},{7,8},{8,9},{9,10},{10,1... | collective-permute-start | bytes 294920 | tf_op jit(solution)/shard_map/ppermute | solution.py:27
  489.8 18.1 %collective-permute-start.20 = (bf16[256,192]{0,1:T(8,128)(2,1)}, bf16[256,192]{0,1:T(8,128)(2,1)}, u32[]{:S(2)}, u32[]{:S(2)}) collective-permute-start(bf16[256,192]{0,1:T(8,128)(2,1)} %bitcast.50), channel_id=1, source_target_pairs={{1,0},{2,1},{3,2},{4,3},{5,4},{6,5},{7,6},{8,7},{9,8},{10,9},{11,1... | collective-permute-start | bytes 294920 | tf_op jit(solution)/shard_map/ppermute | solution.py:27
  493.0 17.2 %collective-permute-start.18 = (bf16[256,192]{0,1:T(8,128)(2,1)}, bf16[256,192]{0,1:T(8,128)(2,1)}, u32[]{:S(2)}, u32[]{:S(2)}) collective-permute-start(bf16[256,192]{0,1:T(8,128)(2,1)} %bitcast.46), channel_id=1, source_target_pairs={{0,1},{1,2},{2,3},{3,4},{4,5},{5,6},{6,7},{7,8},{8,9},{9,10},{10,1... | collective-permute-start | bytes 294920 | tf_op jit(solution)/shard_map/ppermute | solution.py:27
  496.6 18.9 %collective-permute-start.16 = (bf16[256,192]{0,1:T(8,128)(2,1)}, bf16[256,192]{0,1:T(8,128)(2,1)}, u32[]{:S(2)}, u32[]{:S(2)}) collective-permute-start(bf16[256,192]{0,1:T(8,128)(2,1)} %bitcast.44), channel_id=1, source_target_pairs={{1,0},{2,1},{3,2},{4,3},{5,4},{6,5},{7,6},{8,7},{9,8},{10,9},{11,1... | collective-permute-start | bytes 294920 | tf_op jit(solution)/shard_map/ppermute | solution.py:27
  502.8 15.4 %collective-permute-start.23 = (bf16[256,192]{0,1:T(8,128)(2,1)S(1)}, bf16[256,192]{0,1:T(8,128)(2,1)S(1)}, u32[]{:S(2)}, u32[]{:S(2)}) collective-permute-start(bf16[256,192]{0,1:T(8,128)(2,1)S(1)} %fusion.81), channel_id=1, source_target_pairs={{0,1},{1,2},{2,3},{3,4},{4,5},{5,6},{6,7},{7,8},{8,9},{9,10},{10,1... | collective-permute-start | bytes 294920 | tf_op jit(solution)/shard_map/ppermute | solution.py:27
  508.9 9.3 %collective-permute-start.21 = (bf16[256,192]{0,1:T(8,128)(2,1)S(1)}, bf16[256,192]{0,1:T(8,128)(2,1)S(1)}, u32[]{:S(2)}, u32[]{:S(2)}) collective-permute-start(bf16[256,192]{0,1:T(8,128)(2,1)S(1)} %fusion.82), channel_id=1, source_target_pairs={{1,0},{2,1},{3,2},{4,3},{5,4},{6,5},{7,6},{8,7},{9,8},{10,9},{11,1... | collective-permute-start | bytes 294920 | tf_op jit(solution)/shard_map/ppermute | solution.py:27
  537.8 19.4 %collective-permute-start.30 = (bf16[256,192]{0,1:T(8,128)(2,1)}, bf16[256,192]{0,1:T(8,128)(2,1)}, u32[]{:S(2)}, u32[]{:S(2)}) collective-permute-start(bf16[256,192]{0,1:T(8,128)(2,1)} %bitcast.67), channel_id=1, source_target_pairs={{0,1},{1,2},{2,3},{3,4},{4,5},{5,6},{6,7},{7,8},{8,9},{9,10},{10,1... | collective-permute-start | bytes 294920 | tf_op jit(solution)/shard_map/ppermute | solution.py:27
  543.6 20.5 %collective-permute-start.28 = (bf16[256,192]{0,1:T(8,128)(2,1)}, bf16[256,192]{0,1:T(8,128)(2,1)}, u32[]{:S(2)}, u32[]{:S(2)}) collective-permute-start(bf16[256,192]{0,1:T(8,128)(2,1)} %bitcast.65), channel_id=1, source_target_pairs={{1,0},{2,1},{3,2},{4,3},{5,4},{6,5},{7,6},{8,7},{9,8},{10,9},{11,1... | collective-permute-start | bytes 294920 | tf_op jit(solution)/shard_map/ppermute | solution.py:27
  546.4 20.0 %collective-permute-start.26 = (bf16[256,192]{0,1:T(8,128)(2,1)}, bf16[256,192]{0,1:T(8,128)(2,1)}, u32[]{:S(2)}, u32[]{:S(2)}) collective-permute-start(bf16[256,192]{0,1:T(8,128)(2,1)} %bitcast.61), channel_id=1, source_target_pairs={{0,1},{1,2},{2,3},{3,4},{4,5},{5,6},{6,7},{7,8},{8,9},{9,10},{10,1... | collective-permute-start | bytes 294920 | tf_op jit(solution)/shard_map/ppermute | solution.py:27
  550.1 21.5 %collective-permute-start.24 = (bf16[256,192]{0,1:T(8,128)(2,1)}, bf16[256,192]{0,1:T(8,128)(2,1)}, u32[]{:S(2)}, u32[]{:S(2)}) collective-permute-start(bf16[256,192]{0,1:T(8,128)(2,1)} %bitcast.59), channel_id=1, source_target_pairs={{1,0},{2,1},{3,2},{4,3},{5,4},{6,5},{7,6},{8,7},{9,8},{10,9},{11,1... | collective-permute-start | bytes 294920 | tf_op jit(solution)/shard_map/ppermute | solution.py:27
  558.1 15.8 %collective-permute-start.31 = (bf16[256,192]{0,1:T(8,128)(2,1)S(1)}, bf16[256,192]{0,1:T(8,128)(2,1)S(1)}, u32[]{:S(2)}, u32[]{:S(2)}) collective-permute-start(bf16[256,192]{0,1:T(8,128)(2,1)S(1)} %fusion.73), channel_id=1, source_target_pairs={{0,1},{1,2},{2,3},{3,4},{4,5},{5,6},{6,7},{7,8},{8,9},{9,10},{10,1... | collective-permute-start | bytes 294920 | tf_op jit(solution)/shard_map/ppermute | solution.py:27
  565.1 8.8 %collective-permute-start.29 = (bf16[256,192]{0,1:T(8,128)(2,1)S(1)}, bf16[256,192]{0,1:T(8,128)(2,1)S(1)}, u32[]{:S(2)}, u32[]{:S(2)}) collective-permute-start(bf16[256,192]{0,1:T(8,128)(2,1)S(1)} %fusion.74), channel_id=1, source_target_pairs={{1,0},{2,1},{3,2},{4,3},{5,4},{6,5},{7,6},{8,7},{9,8},{10,9},{11,1... | collective-permute-start | bytes 294920 | tf_op jit(solution)/shard_map/ppermute | solution.py:27
  (77 other events, 3436.3 us)
Sparse Core Ops, SparseCore 0:
  579.5 156.4 all-reduce.16
where the time goes:
time: 761 us; the launch traced here: 752 us
  blocking collectives  410 us (54%)
  waiting for transfers between devices  106 us (14%)
  starting transfers between devices  89.1 us (12%)
  other arithmetic  57.1 us (8%)
  local copies, waits for them, and re-layouts  35.9 us (5%)
  matrix products  31.8 us (4%)
  between operations  22.5 us (3%)
    unnamed x2, waiting for transfers between devices  98.8 us
    unnamed x2, blocking collectives  96.4 us
    ppermute x32, starting transfers between devices, shifted(): return lax.ppermute(array, axis, pairs)  89.1 us
    all_gather x2, blocking collectives, local(): lax.all_gather(mlp_out[layer_index], 'dev', axis=0, tiled=True)  80.1 us
    all_gather x2, blocking collectives, local(): lax.all_gather(attn_in[layer_index], 'dev', axis=0, tiled=True)  79.3 us
    all_gather x2, blocking collectives, local(): lax.all_gather(attn_out[layer_index], 'dev', axis=0, tiled=True)  77.9 us
    all_gather x2, blocking collectives, local(): lax.all_gather(mlp_in[layer_index], 'dev', axis=0, tiled=True)  76.5 us
  transfers between devices with their start and end apart: 33, of which 5 were waited for; matrix products, arithmetic and copies ran while one was open for 9% of the time, Pallas kernels for 0%

commit v1 on v0

v1 whole, which is shorter than its diff:
```python
import functools
import math

import jax
import jax.numpy as jnp
import numpy as np
from jax import lax
from jax.experimental import pallas as pl
from jax.experimental.pallas import tpu as pltpu
from jax.sharding import PartitionSpec as P

HD = 64
IMG_LEN = 197
ROWS = 208
IMAGES_HERE = 2
BLOCK = 16
MESH_ID = pl.DeviceIdType.MESH
bf16, f32 = jnp.bfloat16, jnp.float32
eps_norm = 1e-06
masked_fill = -1e30
vmem_bytes = 56 * 2**20


def bit_orders(n):
    count = n.bit_length() - 1
    first = list(range(count))[::-1]
    second = list(first)
    if count >= 3:
        second[-3], second[-2] = second[-2], second[-3]
    return first, second


def slot_of(dev, order, div=lax.div, rem=lax.rem):
    return sum(rem(div(dev, 2**b), 2) * 2**k for k, b in enumerate(order))


def greet(n, me, bits):
    barrier = pltpu.get_barrier_semaphore()
    others = [me + (1 - 2 * lax.rem(lax.div(me, 2**b), 2)) * 2**b for b in range(bits)]
    others += [lax.rem(me + 1, n), lax.rem(me + n - 1, n)]
    for other in others:
        pl.semaphore_signal(barrier, inc=1, device_id=(other,), device_id_type=MESH_ID)
    pl.semaphore_wait(barrier, len(others))
    return others


def remote(src, dst, send, recv, dev):
    return pltpu.make_async_remote_copy(
        src_ref=src, dst_ref=dst, send_sem=send, recv_sem=recv,
        device_id=(dev,), device_id_type=MESH_ID,
    )


def gather_kernel(n, blk_a, blk_b, halo, out_a, out_b, halo_out, send, recv, hsend, hrecv):
    me = lax.axis_index("dev")
    orders = bit_orders(n)
    bits = len(orders[0])
    outs = (out_a, out_b)
    slots = [slot_of(me, order) for order in orders]
    for half, blk in enumerate((blk_a, blk_b)):
        outs[half][pl.ds(slots[half] * BLOCK, BLOCK), :] = blk[...]
    others = greet(n, me, bits)
    halo_copy = remote(halo, halo_out, hsend, hrecv, others[-1])
    halo_copy.start()
    sent = []
    for k in range(bits):
        copies = []
        for half in range(2):
            size = BLOCK * 2**k
            at = pl.ds(pl.multiple_of(lax.div(slots[half], 2**k) * size, BLOCK), size)
            copy = remote(
                outs[half].at[at, :], outs[half].at[at, :],
                send.at[half, k], recv.at[half, k], others[orders[half][k]],
            )
            copy.start()
            copies.append(copy)
        for copy in copies:
            copy.wait_recv()
        sent += copies
    for copy in sent:
        copy.wait_send()
    halo_copy.wait()


def gather(n, blk_a, blk_b, halo):
    bits = n.bit_length() - 1
    width = blk_a.shape[1]
    vm = pl.BlockSpec(memory_space=pltpu.VMEM)
    return pl.pallas_call(
        functools.partial(gather_kernel, n),
        out_shape=(
            jax.ShapeDtypeStruct((n * BLOCK, width), bf16),
            jax.ShapeDtypeStruct((n * BLOCK, width), bf16),
            jax.ShapeDtypeStruct(halo.shape, bf16),
        ),
        in_specs=[vm] * 3,
        out_specs=(vm, vm, vm),
        scratch_shapes=[
            pltpu.SemaphoreType.DMA((2, bits)),
            pltpu.SemaphoreType.DMA((2, bits)),
            pltpu.SemaphoreType.DMA,
            pltpu.SemaphoreType.DMA,
        ],
        compiler_params=pltpu.CompilerParams(
            collective_id=0, has_side_effects=True, vmem_limit_bytes=vmem_bytes
        ),
        name="gather_params",
    )(blk_a, blk_b, halo)


def scatter_kernel(n, s_a, s_b, act, act_up, dx, dx_up,
                   r_a, r_b, act_out, dx_out, *scratch):
    me = lax.axis_index("dev")
    orders = bit_orders(n)
    bits = len(orders[0])
    inbox = [scratch[half * bits:(half + 1) * bits] for half in range(2)]
    outbox = [scratch[(2 + half) * bits:(3 + half) * bits] for half in range(2)]
    totals = [scratch[(4 + half) * bits:(5 + half) * bits] for half in range(2)]
    act_in, dx_in, send, recv, hsend, hrecv = scratch[6 * bits:]
    others = greet(n, me, bits)
    up = others[-2]
    halo = [
        remote(act_up, act_in, hsend.at[0], hrecv.at[0], up),
        remote(dx_up, dx_in, hsend.at[1], hrecv.at[1], up),
    ]
    sources = (s_a, s_b)
    copies = {}

    def bit_at(half, step):
        b = orders[half][bits - 1 - step]
        return b, lax.rem(lax.div(me, 2**b), 2)

    def start(half, step):
        b, bit = bit_at(half, step)
        size = n * BLOCK // 2 ** (step + 1)
        if step == 0:
            src = sources[half].at[pl.ds(pl.multiple_of((1 - bit) * size, BLOCK), size), :]
        else:
            src = outbox[half][step]
        copy = remote(src, inbox[half][step], send.at[half, step], recv.at[half, step], others[b])
        copy.start()
        copies[half, step] = copy

    for half in range(2):
        start(half, 0)
    for copy in halo:
        copy.start()
    for step in range(bits):
        size = n * BLOCK // 2 ** (step + 1)
        for half in range(2):
            copies[half, step].wait_recv()
            _, bit = bit_at(half, step)
            held = sources[half] if step == 0 else totals[half][step - 1]
            base = pl.multiple_of(bit * size, BLOCK)
            if step == bits - 1:
                out = (r_a, r_b)[half]
                out[...] = held[pl.ds(base, size), :].astype(f32) + inbox[half][step][...].astype(f32)
                continue
            _, next_bit = bit_at(half, step + 1)
            part = size // 2
            away = pl.multiple_of((1 - next_bit) * part, BLOCK)
            there = pl.multiple_of(next_bit * part, BLOCK)
            outbox[half][step + 1][...] = (
                held[pl.ds(base + away, part), :].astype(f32)
                + inbox[half][step][pl.ds(away, part), :].astype(f32)
            ).astype(bf16)
            start(half, step + 1)
            totals[half][step][pl.ds(there, part), :] = (
                held[pl.ds(base + there, part), :].astype(f32)
                + inbox[half][step][pl.ds(there, part), :].astype(f32)
            )
    for copy in halo:
        copy.wait_recv()
    act_out[...] = act[...] + act_in[...]
    dx_out[...] = dx[...] + dx_in[...]
    for copy in halo + list(copies.values()):
        copy.wait_send()


def scatter(n, s_a, s_b, act, act_up, dx, dx_up):
    bits = n.bit_length() - 1
    width = s_a.shape[1]
    vm = pl.BlockSpec(memory_space=pltpu.VMEM)
    sizes = [n * BLOCK // 2 ** (step + 1) for step in range(bits)]
    boxes = [pltpu.VMEM((size, width), bf16) for size in sizes]
    totals = [pltpu.VMEM((size, width), f32) for size in sizes]
    return pl.pallas_call(
        functools.partial(scatter_kernel, n),
        out_shape=(
            jax.ShapeDtypeStruct((BLOCK, width), f32),
            jax.ShapeDtypeStruct((BLOCK, width), f32),
            jax.ShapeDtypeStruct(act.shape, act.dtype),
            jax.ShapeDtypeStruct(dx.shape, dx.dtype),
        ),
        in_specs=[vm] * 6,
        out_specs=(vm,) * 4,
        scratch_shapes=boxes * 4 + totals * 2 + [
            pltpu.VMEM(act.shape, act.dtype),
            pltpu.VMEM(dx.shape, dx.dtype),
            pltpu.SemaphoreType.DMA((2, bits)),
            pltpu.SemaphoreType.DMA((2, bits)),
            pltpu.SemaphoreType.DMA((2,)),
            pltpu.SemaphoreType.DMA((2,)),
        ],
        compiler_params=pltpu.CompilerParams(
            collective_id=1, has_side_effects=True, vmem_limit_bytes=vmem_bytes
        ),
        name="scatter_grads",
    )(s_a, s_b, act, act_up, dx, dx_up)


def mm(a, b):
    return jnp.dot(a, b, preferred_element_type=f32)


def mm_nt(a, b):
    return lax.dot_general(a, b, (((1,), (1,)), ((), ())), preferred_element_type=f32)


def mm_tn(a, b):
    return lax.dot_general(a, b, (((0,), (0,)), ((), ())), preferred_element_type=f32)


def norm_forward(x, gain, bias):
    centered = x - jnp.mean(x, axis=-1, keepdims=True)
    inverse = lax.rsqrt(jnp.mean(centered * centered, axis=-1, keepdims=True) + eps_norm)
    hat = centered * inverse
    return (hat * gain + bias).astype(bf16), hat, inverse


def norm_backward(dh, hat, inverse, gain):
    scaled = dh * gain
    dv = inverse * (
        scaled
        - jnp.mean(scaled, axis=-1, keepdims=True)
        - hat * jnp.mean(scaled * hat, axis=-1, keepdims=True)
    )
    return dv, rows_sum(dh * hat), rows_sum(dh)


def rows_sum(x):
    return jnp.sum(x, axis=0, keepdims=True)


def compute_kernel(n, fast, layers, width, hidden_units, ranges, *refs):
    refs = list(refs)
    take = lambda count: [refs.pop(0) for _ in range(count)]
    if fast:
        g_a, g_b, place, perm = take(4)
    else:
        w_full, perm = take(2)
    tok, cot, halo = take(3)
    if fast:
        s_a, s_b = take(2)
    else:
        (grad_out,) = take(1)
    act_own, act_up, dx_own, dx_up = take(4)
    w_all, w_one_s, w_two_s, hat1_s, h1_s, qkv_s, p_s, o_s, hat2_s, h2_s, slope_s, a_s = take(12)
    inv_s, dqkv_s, do_s, grad_s = take(4)
    slots = tok.shape[0]
    heads = width // HD
    d = width
    half_width = 6 * d
    me = lax.axis_index("dev")
    first, last = ranges[me, 0], ranges[me, 1]
    total = ranges[n - 1, 1]
    image = (first + IMG_LEN - 1) // IMG_LEN
    rows = IMAGES_HERE * ROWS

    picks, valid_keys = [], []
    for k in range(IMAGES_HERE):
        begin = (image + k) * IMG_LEN
        count = jnp.where(begin < last, jnp.minimum(IMG_LEN, total - begin), 0)
        r = lax.broadcasted_iota(jnp.int32, (ROWS, 2 * slots), 0)
        c = lax.broadcasted_iota(jnp.int32, (ROWS, 2 * slots), 1)
        t = begin + r
        column = jnp.where(t < last, t - first, t - last + slots)
        column = jnp.where(r < count, column, -1)
        picks.append(jnp.where(column == c, 1.0, 0.0).astype(bf16))
        valid_keys.append(lax.broadcasted_iota(jnp.int32, (ROWS, ROWS), 1) < count)
    pick = jnp.concatenate(picks, axis=0)
    x = mm(pick[:, :slots], tok[...]) + mm(pick[:, slots:], halo[:, :d])

    vec = [None] * layers
    b_one = [None] * layers
    for l in range(layers):
        if fast:
            w_all[l, :, :half_width] = mm(place[0, l], g_a[...]).astype(bf16)
            w_all[l, :, half_width:] = mm(place[1, l], g_b[...]).astype(bf16)
        else:
            w_all[l] = w_full[l]
        w_one_s[l] = mm(w_all[l, :d, 4 * d:8 * d], perm[...]).astype(bf16)
        for j in range(4):
            w_two_s[l, j * d:(j + 1) * d, :] = w_all[l, :d, (8 + j) * d:(9 + j) * d]
        tail = w_all[l, d:d + BLOCK, :]
        vec[l] = tail.astype(f32)[0:1, :]
        b_one[l] = mm(tail[:, 8 * d:], perm[...])[0:1, :]

    def v_of(l, index):
        return vec[l][:, index * d:(index + 1) * d]

    for l in range(layers):
        h, hat, inv = norm_forward(x, v_of(l, 0), v_of(l, 1))
        hat1_s[l], h1_s[l], inv_s[l, 0] = hat, h, inv
        projected = mm(h, w_all[l, :d, :3 * d])
        qkv_s[l, :, :d] = ((projected[:, :d] + v_of(l, 2)).astype(bf16).astype(f32)
                           * (1.0 / math.sqrt(HD))).astype(bf16)
        qkv_s[l, :, d:2 * d] = projected[:, d:2 * d].astype(bf16)
        qkv_s[l, :, 2 * d:] = (projected[:, 2 * d:] + v_of(l, 3)).astype(bf16)
        for i in range(IMAGES_HERE):
            at = slice(i * ROWS, (i + 1) * ROWS)
            for head in range(heads):
                q = qkv_s[l, at, head * HD:(head + 1) * HD]
                key = qkv_s[l, at, d + head * HD:d + (head + 1) * HD]
                val = qkv_s[l, at, 2 * d + head * HD:2 * d + (head + 1) * HD]
                scores = jnp.where(valid_keys[i], mm_nt(q, key), masked_fill)
                e = jnp.exp(scores - jnp.max(scores, axis=-1, keepdims=True))
                p = e * (1.0 / jnp.sum(e, axis=-1, keepdims=True))
                p_s[l, i, head] = p
                o_s[l, at, head * HD:(head + 1) * HD] = mm(p.astype(bf16), val).astype(bf16)
        x1 = x + (mm(o_s[l], w_all[l, :d, 3 * d:4 * d]) + v_of(l, 4))
        h2, hat, inv = norm_forward(x1, v_of(l, 5), v_of(l, 6))
        hat2_s[l], h2_s[l], inv_s[l, 1] = hat, h2, inv
        u = mm(h2, w_one_s[l]) + b_one[l]
        phi = 0.5 * (1.0 + lax.erf(u * (1.0 / math.sqrt(2.0))))
        a_s[l] = (u * phi).astype(bf16)
        slope_s[l] = phi + u * (jnp.exp(-0.5 * u * u) * (1.0 / math.sqrt(2.0 * math.pi)))
        x = x1 + (mm(a_s[l], w_two_s[l]) + v_of(l, 7))

    x_low = x.astype(bf16)
    act_own[...] = mm_tn(pick[:, :slots], x_low).astype(bf16)
    act_up[...] = mm_tn(pick[:, slots:], x_low).astype(bf16)

    dx = mm(pick[:, :slots], cot[...]) + mm(pick[:, slots:], halo[:, d:])
    for l in reversed(range(layers)):
        dm = dx.astype(bf16)
        g_two = mm_tn(a_s[l], dm)
        for j in range(4):
            grad_s[l, :d, (8 + j) * d:(9 + j) * d] = g_two[j * d:(j + 1) * d, :].astype(bf16)
        g_b2 = rows_sum(dm.astype(f32))
        du = (mm_nt(dm, w_two_s[l]) * slope_s[l]).astype(bf16)
        g_b1 = mm_nt(jnp.broadcast_to(rows_sum(du.astype(f32)), (BLOCK, hidden_units)).astype(bf16),
                     perm[...])[0:1, :]
        g_one = mm_tn(h2_s[l], du).astype(bf16)
        grad_s[l, :d, 4 * d:8 * d] = mm_nt(g_one, perm[...]).astype(bf16)
        dh2 = mm_nt(du, w_one_s[l])
        dv, g_g2, g_c2 = norm_backward(dh2, hat2_s[l], inv_s[l, 1], v_of(l, 5))
        dx1 = dx + dv
        db = dx1.astype(bf16)
        g_bo = rows_sum(db.astype(f32))
        grad_s[l, :d, 3 * d:4 * d] = mm_tn(o_s[l], db).astype(bf16)
        do_s[...] = mm_nt(db, w_all[l, :d, 3 * d:4 * d]).astype(bf16)
        for i in range(IMAGES_HERE):
            at = slice(i * ROWS, (i + 1) * ROWS)
            for head in range(heads):
                q_at = slice(head * HD, (head + 1) * HD)
                k_at = slice(d + head * HD, d + (head + 1) * HD)
                v_at = slice(2 * d + head * HD, 2 * d + (head + 1) * HD)
                do = do_s[at, q_at]
                p = p_s[l, i, head]
                dp = mm_nt(do, qkv_s[l, at, v_at])
                ds = (p * (dp - jnp.sum(p * dp, axis=-1, keepdims=True))).astype(bf16)
                dqkv_s[at, q_at] = (mm(ds, qkv_s[l, at, k_at]) * (1.0 / math.sqrt(HD))).astype(bf16)
                dqkv_s[at, k_at] = mm_tn(ds, qkv_s[l, at, q_at]).astype(bf16)
                dqkv_s[at, v_at] = mm_tn(p.astype(bf16), do).astype(bf16)
        g_bq = rows_sum(dqkv_s[:, :d].astype(f32))
        g_bv = rows_sum(dqkv_s[:, 2 * d:].astype(f32))
        grad_s[l, :d, :3 * d] = mm_tn(h1_s[l], dqkv_s[...]).astype(bf16)
        dh = mm_nt(dqkv_s[...], w_all[l, :d, :3 * d])
        dv, g_g1, g_c1 = norm_backward(dh, hat1_s[l], inv_s[l, 0], v_of(l, 0))
        dx = dx1 + dv
        line = jnp.concatenate([g_g1, g_c1, g_bq, g_bv, g_bo, g_g2, g_c2, g_b2, g_b1], axis=1)
        grad_s[l, d:d + BLOCK, :] = jnp.broadcast_to(line, (BLOCK, line.shape[1])).astype(bf16)

    high = dx.astype(bf16)
    low = (dx - high.astype(f32)).astype(bf16)
    dx_own[...] = mm_tn(pick[:, :slots], high) + mm_tn(pick[:, :slots], low)
    dx_up[...] = mm_tn(pick[:, slots:], high) + mm_tn(pick[:, slots:], low)
    if fast:
        for half, out in enumerate((s_a, s_b)):
            cols = slice(half * half_width, (half + 1) * half_width)
            part = mm_tn(place[half, 0], grad_s[0, :, cols])
            for l in range(1, layers):
                part += mm_tn(place[half, l], grad_s[l, :, cols])
            out[...] = part.astype(bf16)
    else:
        grad_out[...] = grad_s[...]


def compute(n, fast, ranges, weights, tok, cot, halo, layers):
    slots, d = tok.shape
    hidden_units = 4 * d
    rows = IMAGES_HERE * ROWS
    tall = d + BLOCK
    wide = 12 * d
    unit = np.arange(hidden_units)
    perm = np.zeros((hidden_units, hidden_units), np.float32)
    perm[unit, (unit % 4) * d + unit // 4] = 1.0
    args = list(weights)
    if fast:
        per = d // n
        place = np.zeros((2, layers, tall, n * BLOCK), np.float32)
        for half, order in enumerate(bit_orders(n)):
            for dev in range(n):
                at = slot_of(dev, order, lambda a, b: a // b, lambda a, b: a % b) * BLOCK
                for l in range(layers):
                    for i in range(per):
                        place[half, l, dev * per + i, at + l * per + i] = 1.0
                    place[half, l, d, at + layers * per + l] = 1.0
        args.append(jnp.asarray(place, bf16))
        outs = [jax.ShapeDtypeStruct((n * BLOCK, wide // 2), bf16)] * 2
    else:
        outs = [jax.ShapeDtypeStruct((layers, tall, wide), bf16)]
    args += [jnp.asarray(perm, bf16), tok, cot, halo]
    outs += [jax.ShapeDtypeStruct((slots, d), bf16)] * 2 + [jax.ShapeDtypeStruct((slots, d), f32)] * 2
    vm = pl.BlockSpec(memory_space=pltpu.VMEM)
    return pl.pallas_call(
        functools.partial(compute_kernel, n, fast, layers, d, hidden_units),
        out_shape=tuple(outs),
        in_specs=[pl.BlockSpec(memory_space=pltpu.SMEM)] + [vm] * len(args),
        out_specs=(vm,) * len(outs),
        scratch_shapes=[
            pltpu.VMEM((layers, tall, wide), bf16),
            pltpu.VMEM((layers, d, hidden_units), bf16),
            pltpu.VMEM((layers, hidden_units, d), bf16),
            pltpu.VMEM((layers, rows, d), f32),
            pltpu.VMEM((layers, rows, d), bf16),
            pltpu.VMEM((layers, rows, 3 * d), bf16),
            pltpu.VMEM((layers, IMAGES_HERE, d // HD, ROWS, ROWS), f32),
            pltpu.VMEM((layers, rows, d), bf16),
            pltpu.VMEM((layers, rows, d), f32),
            pltpu.VMEM((layers, rows, d), bf16),
            pltpu.VMEM((layers, rows, hidden_units), f32),
            pltpu.VMEM((layers, rows, hidden_units), bf16),
            pltpu.VMEM((layers, 2, rows, 1), f32),
            pltpu.VMEM((rows, 3 * d), bf16),
            pltpu.VMEM((rows, d), bf16),
            pltpu.VMEM((layers, tall, wide), bf16),
        ],
        compiler_params=pltpu.CompilerParams(vmem_limit_bytes=vmem_bytes),
        name="two_layers",
    )(ranges, *args)


def rows_of(flats, d):
    w_in, w_out, w_one, w_two = flats
    layers = w_in.shape[0]
    return jnp.concatenate(
        [
            w_in.reshape(layers, -1, 3 * d),
            w_out.reshape(layers, -1, d),
            w_one.reshape(layers, -1, 4 * d),
            w_two.reshape(layers, -1, 4 * d),
        ],
        axis=2,
    )


def flats_of(block, d):
    layers = block.shape[0]
    ends = (0, 3 * d, 4 * d, 8 * d, 12 * d)
    return [block[:, :, lo:hi].reshape(layers, -1) for lo, hi in zip(ends, ends[1:])]


def local(tokens, ranges, attn_in, attn_out, mlp_in, mlp_out, vectors, cotangent):
    n = lax.axis_size("dev")
    me = lax.axis_index("dev")
    slots, d = tokens.shape
    layers, part = vectors.shape
    flats = (attn_in, attn_out, mlp_in, mlp_out)
    halo = jnp.concatenate([tokens, cotangent], axis=1)
    fast = d % n == 0 and n & (n - 1) == 0 and layers * (d // n + 1) <= BLOCK and n >= 8
    if fast:
        per = d // n
        block = rows_of(flats, d).reshape(layers * per, 12 * d)
        line = jnp.zeros((layers, 12 * d), bf16)
        line = lax.dynamic_update_slice(line, vectors, (0, me * part))
        spare = jnp.zeros((BLOCK - layers * (per + 1), 12 * d), bf16)
        block = jnp.concatenate([block, line, spare], axis=0)
        g_a, g_b, halo_in = gather(n, block[:, :6 * d], block[:, 6 * d:], halo)
        s_a, s_b, act, act_up, dx, dx_up = compute(
            n, True, ranges, (g_a, g_b), tokens, cotangent, halo_in, layers
        )
        r_a, r_b, act, dx = scatter(n, s_a, s_b, act, act_up, dx, dx_up)
        full = jnp.concatenate([r_a, r_b], axis=1)
        grads = flats_of(full[:layers * per].reshape(layers, per, 12 * d), d)
        lines = full[layers * per:layers * (per + 1)]
        grads.append(lax.dynamic_slice(lines, (0, me * part), (layers, part)))
    else:
        whole = [
            jnp.stack([lax.all_gather(flat[l], "dev", axis=0, tiled=True) for l in range(layers)])
            for flat in flats + (vectors,)
        ]
        line = whole.pop()
        spare = jnp.zeros((layers, BLOCK - 1, 12 * d), bf16)
        block = jnp.concatenate([rows_of(whole, d), line[:, None, :], spare], axis=1)
        halo_in = lax.ppermute(halo, "dev", [(i, (i + n - 1) % n) for i in range(n)])
        grad, act, act_up, dx, dx_up = compute(
            n, False, ranges, (block,), tokens, cotangent, halo_in, layers
        )
        up = [(i, (i + 1) % n) for i in range(n)]
        act = act + lax.ppermute(act_up, "dev", up)
        dx = dx + lax.ppermute(dx_up, "dev", up)
        terms = flats_of(grad[:, :d], d) + [grad[:, d]]
        grads = [
            jnp.stack([
                lax.psum_scatter(term[l].astype(f32), "dev", scatter_dimension=0, tiled=True)
                for l in range(layers)
            ])
            for term in terms
        ]
    return (act, dx, *grads)


def solution(mesh):
    flat = P(None, "dev")
    rows = P("dev", None)
    return jax.shard_map(
        local,
        mesh=mesh,
        in_specs=(rows, P(), flat, flat, flat, flat, flat, rows),
        out_specs=(rows, rows, flat, flat, flat, flat, flat),
        check_vma=False,
    )
```

time: 761 us -> 105 us (0.14); the launches traced: 752 us -> 105 us
  blocking collectives: 410 us -> 0 us
  waiting for transfers between devices: 106 us -> 0 us
  starting transfers between devices: 89.1 us -> 0 us
  Pallas kernels: 0 us -> 87.7 us
  other arithmetic: 57.1 us -> 0.82 us
  matrix products: 31.8 us -> 0 us
  between operations: 22.5 us -> 0.75 us
  local copies, waits for them, and re-layouts: 35.9 us -> 15.7 us
    all_gather x8 -> x0, blocking collectives: 314 us -> none  [the longest x2 80.1 us: local(): lax.all_gather(mlp_out[layer_index], 'dev', axis=0, tiled=True)]
    unnamed x2 -> x0, waiting for transfers between devices: 98.8 us -> none
    unnamed x2 -> x0, blocking collectives: 96.4 us -> none
    ppermute x32 -> x0, starting transfers between devices: 89.1 us -> none  [shifted(): return lax.ppermute(array, axis, pairs)]
    pallas_call x0 -> x3, Pallas kernels: none -> 87.7 us  [the longest x1 33.7 us: scatter(): pl.pallas_call(functools.partial(scatter_kernel, n), out_shape=(jax.Shape...]
    dot_general x36 -> x0, matrix products: 31.8 us -> none  [the longest x2 4.78 us: layer_forward(): jnp.dot(normed_two_low, w_one, preferred_element_type=jnp.float32)]
    all_gather x8 -> x0, other arithmetic: 27.9 us -> none  [the longest x2 12.2 us: local(): lax.all_gather(mlp_in[layer_index], 'dev', axis=0, tiled=True)]
    convert_element_type x16 -> x0, other arithmetic: 13.6 us -> none  [the longest x8 7.82 us: short(): return part.astype(jnp.bfloat16) if part.dtype == jnp.float32 else part]
  transfers between devices with their start and end apart: 33 -> 0, of which waited for: 5 -> 0; matrix products, arithmetic and copies ran while one was open for 9% -> 0% of each run, Pallas kernels for 0% -> 0%
where the time goes in v1:
time: 105 us
  Pallas kernels  87.7 us (84%)
  local copies, waits for them, and re-layouts  15.7 us (15%)
    pallas_call x1, Pallas kernels, scatter(): pl.pallas_call(functools.partial(scatter_kernel, n), out_shape=(jax.Shape...  33.7 us
    pallas_call x1, Pallas kernels, gather(): pl.pallas_call(functools.partial(gather_kernel, n), out_shape=(jax.ShapeD...  31.4 us
    pallas_call x1, Pallas kernels, compute(): pl.pallas_call(functools.partial(compute_kernel, n, fast, layers, d, hidd...  22.7 us
    unnamed x15, local copies, waits for them, and re-layouts  8.06 us
    concatenate x5, local copies, waits for them, and re-layouts, rows_of(): jnp.concatenate([w_in.reshape(layers, -1, 3 * d), w_out.reshape(layers, -...  3.15 us

profile of v1, /device:TPU:0, one launch (start us, length us, event | category | flops | bytes accessed | tf_op | source)
XLA Modules:
  0.0 104.9 jit_solution(17559123225800027592)
XLA Ops:
  0.6 0.8 concatenate.22
  1.4 0.8 dynamic_update_slice.3
  2.2 1.4 %copy.26.ranges = s32[32,2]{1,0:T(8,128)} copy(s32[32,2]{0,1:T(2,128)} %param.11) | data formatting | bytes 512 | tf_op args[1]
  3.6 0.8 concatenate.21
  4.4 0.7 concatenate.23
  5.1 0.7 concatenate.24
  5.9 0.1 concatenate.25
  6.0 0.6 fusion
  6.7 1.0 copy.24.refs_4_
  7.7 1.0 copy.25.refs_5_
  8.7 0.8 pad_maximum_fusion.halo
  9.5 31.4 %gather_params.1 = (bf16[512,1152]{1,0:T(8,128)(2,1)}, bf16[512,1152]{1,0:T(8,128)(2,1)}, bf16[256,384]{1,0:T(8,128)(2,1)}) custom-call(bf16[16,1152]{1,0:T(8,128)(2,1)} %get-tuple-element.50.blk_a, bf16[16,1152]{1,0:T(8,128)(2,1)} %get-tuple-element.49.blk_b, bf16[256,384]{1,0:T(8,128)(2,1)} %pad_maximum_fusion.halo), custom_call_target="tpu_custom_call" | custom-call | tf_op jit(solution)/shard_map/gather_params/pallas_call | solution.py:89
  40.9 22.7 %two_layers.1 = (bf16[512,1152]{1,0:T(8,128)(2,1)}, bf16[512,1152]{1,0:T(8,128)(2,1)}, bf16[256,192]{1,0:T(8,128)(2,1)}, bf16[256,192]{1,0:T(8,128)(2,1)}, f32[256,192]{1,0:T(8,128)}, /*index=5*/f32[256,192]{1,0:T(8,128)}) custom-call(s32[32,2]{1,0:T(8,128)} %copy.26.ranges, bf16[512,1152]{1,0:T(8,128)(2,1)} %get-tuple-element.20.refs_0_, ...), custom_call_target="tpu_custom_call" | custom-call | tf_op jit(solution)/shard_map/two_layers/pallas_call | solution.py:417
  63.5 33.7 %scatter_grads.1 = (f32[16,1152]{1,0:T(8,128)}, f32[16,1152]{1,0:T(8,128)}, bf16[256,192]{1,0:T(8,128)(2,1)}, f32[256,192]{1,0:T(8,128)}) custom-call(bf16[512,1152]{1,0:T(8,128)(2,1)} %get-tuple-element.23.s_a, bf16[512,1152]{1,0:T(8,128)(2,1)} %get-tuple-element.24.s_b, bf16[256,192]{1,0:T(8,128)(2,1)} %get-tuple-element.25.act, ...), custom_call_target="tpu_custom_call" | custom-call | tf_op jit(solution)/shard_map/scatter_grads/pallas_call | solution.py:187
  97.2 1.7 %copy.29 = bf16[256,192]{0,1:T(8,128)(2,1)} copy(bf16[256,192]{1,0:T(8,128)(2,1)} %get-tuple-element.40) | data formatting | bytes 196608
  98.9 0.9 constant_dynamic-update-slice_fusion.1
  99.8 0.9 constant_dynamic-update-slice_fusion
  100.7 0.6 constant_dynamic-slice_fusion
  101.4 0.1 slice.36
  101.4 0.7 reshape.44
  102.1 0.7 reshape.43
  102.8 0.6 copy.32
  103.5 0.6 copy.31
  104.1 0.8 copy.30
  (13 shorter events, 0.1 us)
Async XLA Ops:
  7.6 33.2 %copy-start = (bf16[256,192]{1,0:T(8,128)(2,1)}, bf16[256,192]{1,0:T(8,128)(2,1)S(1)}, u32[]{:S(2)}) copy-start(bf16[256,192]{1,0:T(8,128)(2,1)S(1)} %copy.24.refs_4_) | copy-start | bytes 294916
  8.7 32.2 %copy-start.1 = (bf16[256,192]{1,0:T(8,128)(2,1)}, bf16[256,192]{1,0:T(8,128)(2,1)S(1)}, u32[]{:S(2)}) copy-start(bf16[256,192]{1,0:T(8,128)(2,1)S(1)} %copy.25.refs_5_) | copy-start | bytes 294916
  97.2 6.9 %copy-start.2 = (f32[256,192]{1,0:T(8,128)S(1)}, f32[256,192]{1,0:T(8,128)}, u32[]{:S(2)}) copy-start(f32[256,192]{1,0:T(8,128)} %get-tuple-element.41) | copy-start | bytes 589828

commit v2 on v1

--- a/solution.py
+++ b/solution.py
@@ -3,7 +3,6 @@
 
 import jax
 import jax.numpy as jnp
-import numpy as np
 from jax import lax
 from jax.experimental import pallas as pl
 from jax.experimental.pallas import tpu as pltpu
@@ -21,13 +20,15 @@
 vmem_bytes = 56 * 2**20
 
 
+PIECES = 6
+
+
 def bit_orders(n):
-    count = n.bit_length() - 1
-    first = list(range(count))[::-1]
-    second = list(first)
-    if count >= 3:
-        second[-3], second[-2] = second[-2], second[-3]
-    return first, second
+    down = list(range(n.bit_length() - 1))[::-1]
+    lead, (p, q, r, s) = down[:-4], down[-4:]
+    first, second = lead + [p, q, r, s], lead + [p, r, q, s]
+    third, fourth = lead + [q, r, p, s], lead + [r, q, p, s]
+    return first, second, third, first, second, fourth
 
 
 def slot_of(dev, order, div=lax.div, rem=lax.rem):
@@ -51,79 +52,85 @@
     )
 
 
-def gather_kernel(n, blk_a, blk_b, halo, out_a, out_b, halo_out, send, recv, hsend, hrecv):
+def gather_kernel(n, blk, tok, cot, *refs):
+    outs, (tok_out, cot_out, send, recv, hsend, hrecv) = refs[:PIECES], refs[PIECES:]
     me = lax.axis_index("dev")
     orders = bit_orders(n)
     bits = len(orders[0])
-    outs = (out_a, out_b)
     slots = [slot_of(me, order) for order in orders]
-    for half, blk in enumerate((blk_a, blk_b)):
-        outs[half][pl.ds(slots[half] * BLOCK, BLOCK), :] = blk[...]
+    width = outs[0].shape[1]
+    for c in range(PIECES):
+        outs[c][pl.ds(slots[c] * BLOCK, BLOCK), :] = blk[:, c * width:(c + 1) * width]
     others = greet(n, me, bits)
-    halo_copy = remote(halo, halo_out, hsend, hrecv, others[-1])
-    halo_copy.start()
     sent = []
     for k in range(bits):
         copies = []
-        for half in range(2):
+        for c in range(PIECES):
+            if k:
+                sent[-PIECES].wait_recv()
             size = BLOCK * 2**k
-            at = pl.ds(pl.multiple_of(lax.div(slots[half], 2**k) * size, BLOCK), size)
+            at = pl.ds(pl.multiple_of(lax.div(slots[c], 2**k) * size, BLOCK), size)
             copy = remote(
-                outs[half].at[at, :], outs[half].at[at, :],
-                send.at[half, k], recv.at[half, k], others[orders[half][k]],
+                outs[c].at[at, :], outs[c].at[at, :],
+                send.at[c, k], recv.at[c, k], others[orders[c][k]],
             )
             copy.start()
-            copies.append(copy)
-        for copy in copies:
-            copy.wait_recv()
-        sent += copies
+            sent.append(copy)
+        if k == 0:
+            halo = [
+                remote(tok, tok_out, hsend.at[0], hrecv.at[0], others[-1]),
+                remote(cot, cot_out, hsend.at[1], hrecv.at[1], others[-1]),
+            ]
+            for copy in halo:
+                copy.start()
+    for copy in sent[-PIECES:]:
+        copy.wait_recv()
     for copy in sent:
         copy.wait_send()
-    halo_copy.wait()
-
-
-def gather(n, blk_a, blk_b, halo):
+    for copy in halo:
+        copy.wait()
+
+
+def gather(n, blk, tok, cot):
     bits = n.bit_length() - 1
-    width = blk_a.shape[1]
+    width = blk.shape[1] // PIECES
     vm = pl.BlockSpec(memory_space=pltpu.VMEM)
     return pl.pallas_call(
         functools.partial(gather_kernel, n),
-        out_shape=(
-            jax.ShapeDtypeStruct((n * BLOCK, width), bf16),
-            jax.ShapeDtypeStruct((n * BLOCK, width), bf16),
-            jax.ShapeDtypeStruct(halo.shape, bf16),
-        ),
+        out_shape=(jax.ShapeDtypeStruct((n * BLOCK, width), bf16),) * PIECES
+        + (jax.ShapeDtypeStruct(tok.shape, bf16),) * 2,
         in_specs=[vm] * 3,
-        out_specs=(vm, vm, vm),
+        out_specs=(vm,) * (PIECES + 2),
         scratch_shapes=[
-            pltpu.SemaphoreType.DMA((2, bits)),
-            pltpu.SemaphoreType.DMA((2, bits)),
-            pltpu.SemaphoreType.DMA,
-            pltpu.SemaphoreType.DMA,
+            pltpu.SemaphoreType.DMA((PIECES, bits)),
+            pltpu.SemaphoreType.DMA((PIECES, bits)),
+            pltpu.SemaphoreType.DMA((2,)),
+            pltpu.SemaphoreType.DMA((2,)),
         ],
         compiler_params=pltpu.CompilerParams(
             collective_id=0, has_side_effects=True, vmem_limit_bytes=vmem_bytes
         ),
         name="gather_params",
-    )(blk_a, blk_b, halo)
-
-
-def scatter_kernel(n, s_a, s_b, act, act_up, dx, dx_up,
-                   r_a, r_b, act_out, dx_out, *scratch):
+    )(blk, tok, cot)
+
+
+def scatter_kernel(n, *refs):
+    sources, refs = refs[:PIECES], refs[PIECES:]
+    act, act_up, dx, dx_up, result, act_out, dx_out = refs[:7]
+    scratch = refs[7:]
     me = lax.axis_index("dev")
     orders = bit_orders(n)
     bits = len(orders[0])
-    inbox = [scratch[half * bits:(half + 1) * bits] for half in range(2)]
-    outbox = [scratch[(2 + half) * bits:(3 + half) * bits] for half in range(2)]
-    totals = [scratch[(4 + half) * bits:(5 + half) * bits] for half in range(2)]
-    act_in, dx_in, send, recv, hsend, hrecv = scratch[6 * bits:]
+    width = sources[0].shape[1]
+    groups = [scratch[k * bits:(k + 1) * bits] for k in range(3 * PIECES)]
+    inbox, outbox, totals = groups[:PIECES], groups[PIECES:2 * PIECES], groups[2 * PIECES:]
+    act_in, dx_in, send, recv, hsend, hrecv = scratch[3 * PIECES * bits:]
     others = greet(n, me, bits)
     up = others[-2]
     halo = [
         remote(act_up, act_in, hsend.at[0], hrecv.at[0], up),
         remote(dx_up, dx_in, hsend.at[1], hrecv.at[1], up),
     ]
-    sources = (s_a, s_b)
     copies = {}
 
     def bit_at(half, step):
@@ -141,20 +148,19 @@
         copy.start()
         copies[half, step] = copy
 
-    for half in range(2):
+    for half in range(PIECES):
         start(half, 0)
     for copy in halo:
         copy.start()
     for step in range(bits):
         size = n * BLOCK // 2 ** (step + 1)
-        for half in range(2):
+        for half in range(PIECES):
             copies[half, step].wait_recv()
             _, bit = bit_at(half, step)
             held = sources[half] if step == 0 else totals[half][step - 1]
             base = pl.multiple_of(bit * size, BLOCK)
             if step == bits - 1:
-                out = (r_a, r_b)[half]
-                out[...] = held[pl.ds(base, size), :].astype(f32) + inbox[half][step][...].astype(f32)
+                result[:, half * width:(half + 1) * width] = held[pl.ds(base, size), :].astype(f32) + inbox[half][step][...].astype(f32)
                 continue
             _, next_bit = bit_at(half, step + 1)
             part = size // 2
@@ -177,9 +183,9 @@
         copy.wait_send()
 
 
-def scatter(n, s_a, s_b, act, act_up, dx, dx_up):
+def scatter(n, parts, act, act_up, dx, dx_up):
     bits = n.bit_length() - 1
-    width = s_a.shape[1]
+    width = parts[0].shape[1]
     vm = pl.BlockSpec(memory_space=pltpu.VMEM)
     sizes = [n * BLOCK // 2 ** (step + 1) for step in range(bits)]
     boxes = [pltpu.VMEM((size, width), bf16) for size in sizes]
@@ -187,18 +193,17 @@
     return pl.pallas_call(
         functools.partial(scatter_kernel, n),
         out_shape=(
-            jax.ShapeDtypeStruct((BLOCK, width), f32),
-            jax.ShapeDtypeStruct((BLOCK, width), f32),
+            jax.ShapeDtypeStruct((BLOCK, PIECES * width), f32),
             jax.ShapeDtypeStruct(act.shape, act.dtype),
             jax.ShapeDtypeStruct(dx.shape, dx.dtype),
         ),
-        in_specs=[vm] * 6,
-        out_specs=(vm,) * 4,
-        scratch_shapes=boxes * 4 + totals * 2 + [
+        in_specs=[vm] * (PIECES + 4),
+        out_specs=(vm,) * 3,
+        scratch_shapes=boxes * (2 * PIECES) + totals * PIECES + [
             pltpu.VMEM(act.shape, act.dtype),
             pltpu.VMEM(dx.shape, dx.dtype),
-            pltpu.SemaphoreType.DMA((2, bits)),
-            pltpu.SemaphoreType.DMA((2, bits)),
+            pltpu.SemaphoreType.DMA((PIECES, bits)),
+            pltpu.SemaphoreType.DMA((PIECES, bits)),
             pltpu.SemaphoreType.DMA((2,)),
             pltpu.SemaphoreType.DMA((2,)),
         ],
@@ -206,7 +211,7 @@
             collective_id=1, has_side_effects=True, vmem_limit_bytes=vmem_bytes
         ),
         name="scatter_grads",
-    )(s_a, s_b, act, act_up, dx, dx_up)
+    )(*parts, act, act_up, dx, dx_up)
 
 
 def mm(a, b):
@@ -246,21 +251,20 @@
     refs = list(refs)
     take = lambda count: [refs.pop(0) for _ in range(count)]
     if fast:
-        g_a, g_b, place, perm = take(4)
+        pieces = take(PIECES)
     else:
-        w_full, perm = take(2)
-    tok, cot, halo = take(3)
+        (w_full,) = take(1)
+    tok, cot, tok_up, cot_up = take(4)
     if fast:
-        s_a, s_b = take(2)
+        parts = take(PIECES)
     else:
         (grad_out,) = take(1)
     act_own, act_up, dx_own, dx_up = take(4)
     w_all, w_one_s, w_two_s, hat1_s, h1_s, qkv_s, p_s, o_s, hat2_s, h2_s, slope_s, a_s = take(12)
-    inv_s, dqkv_s, do_s, grad_s = take(4)
+    inv_s, dqkv_s, do_s, grad_s, perm = take(5)
     slots = tok.shape[0]
     heads = width // HD
     d = width
-    half_width = 6 * d
     me = lax.axis_index("dev")
     first, last = ranges[me, 0], ranges[me, 1]
     total = ranges[n - 1, 1]
@@ -279,14 +283,36 @@
         picks.append(jnp.where(column == c, 1.0, 0.0).astype(bf16))
         valid_keys.append(lax.broadcasted_iota(jnp.int32, (ROWS, ROWS), 1) < count)
     pick = jnp.concatenate(picks, axis=0)
-    x = mm(pick[:, :slots], tok[...]) + mm(pick[:, slots:], halo[:, :d])
+    x = mm(pick[:, :slots], tok[...]) + mm(pick[:, slots:], tok_up[...])
+
+    unit = lax.broadcasted_iota(jnp.int32, (1, hidden_units), 1)
+    group = sum(jnp.where(unit >= j * d, 1, 0) for j in range(1, 4))
+    origin = 4 * (unit - group * d) + group
+    f = lax.broadcasted_iota(jnp.int32, (hidden_units, hidden_units), 0)
+    perm[...] = jnp.where(f == origin, 1.0, 0.0).astype(bf16)
+    if fast:
+        (place_s,) = take(1)
+        per = d // n
+        orders = bit_orders(n)
+        kinds = [orders[:c + 1].index(order) for c, order in enumerate(orders)]
+        c = lax.broadcasted_iota(jnp.int32, (1, n * BLOCK), 1)
+        line = lax.broadcasted_iota(jnp.int32, (d + BLOCK, n * BLOCK), 0)
+        inside = c & (BLOCK - 1)
+        for kind in set(kinds):
+            dev = sum(((c >> (4 + k)) & 1) << b for k, b in enumerate(orders[kind]))
+            for l in range(layers):
+                row = inside - l * per
+                goal = jnp.where((row >= 0) & (row < per), dev * per + row, -1)
+                goal = jnp.where(inside == layers * per + l, d, goal)
+                place_s[kind, l] = jnp.where(line == goal, 1.0, 0.0).astype(bf16)
 
     vec = [None] * layers
     b_one = [None] * layers
     for l in range(layers):
         if fast:
-            w_all[l, :, :half_width] = mm(place[0, l], g_a[...]).astype(bf16)
-            w_all[l, :, half_width:] = mm(place[1, l], g_b[...]).astype(bf16)
+            for c, piece in enumerate(pieces):
+                cols = slice(c * piece.shape[1], (c + 1) * piece.shape[1])
+                w_all[l, :, cols] = mm(place_s[kinds[c], l], piece[...]).astype(bf16)
         else:
             w_all[l] = w_full[l]
         w_one_s[l] = mm(w_all[l, :d, 4 * d:8 * d], perm[...]).astype(bf16)
@@ -331,7 +357,7 @@
     act_own[...] = mm_tn(pick[:, :slots], x_low).astype(bf16)
     act_up[...] = mm_tn(pick[:, slots:], x_low).astype(bf16)
 
-    dx = mm(pick[:, :slots], cot[...]) + mm(pick[:, slots:], halo[:, d:])
+    dx = mm(pick[:, :slots], cot[...]) + mm(pick[:, slots:], cot_up[...])
     for l in reversed(range(layers)):
         dm = dx.astype(bf16)
         g_two = mm_tn(a_s[l], dm)
@@ -377,41 +403,29 @@
     dx_own[...] = mm_tn(pick[:, :slots], high) + mm_tn(pick[:, :slots], low)
     dx_up[...] = mm_tn(pick[:, slots:], high) + mm_tn(pick[:, slots:], low)
     if fast:
-        for half, out in enumerate((s_a, s_b)):
-            cols = slice(half * half_width, (half + 1) * half_width)
-            part = mm_tn(place[half, 0], grad_s[0, :, cols])
+        for c, out in enumerate(parts):
+            cols = slice(c * out.shape[1], (c + 1) * out.shape[1])
+            part = mm_tn(place_s[kinds[c], 0], grad_s[0, :, cols])
             for l in range(1, layers):
-                part += mm_tn(place[half, l], grad_s[l, :, cols])
+                part += mm_tn(place_s[kinds[c], l], grad_s[l, :, cols])
             out[...] = part.astype(bf16)
     else:
         grad_out[...] = grad_s[...]
 
 
-def compute(n, fast, ranges, weights, tok, cot, halo, layers):
+def compute(n, fast, ranges, weights, tok, cot, tok_up, cot_up, layers):
     slots, d = tok.shape
     hidden_units = 4 * d
     rows = IMAGES_HERE * ROWS
     tall = d + BLOCK
     wide = 12 * d
-    unit = np.arange(hidden_units)
-    perm = np.zeros((hidden_units, hidden_units), np.float32)
-    perm[unit, (unit % 4) * d + unit // 4] = 1.0
-    args = list(weights)
+    args = list(weights) + [tok, cot, tok_up, cot_up]
     if fast:
-        per = d // n
-        place = np.zeros((2, layers, tall, n * BLOCK), np.float32)
-        for half, order in enumerate(bit_orders(n)):
-            for dev in range(n):
-                at = slot_of(dev, order, lambda a, b: a // b, lambda a, b: a % b) * BLOCK
-                for l in range(layers):
-                    for i in range(per):
-                        place[half, l, dev * per + i, at + l * per + i] = 1.0
-                    place[half, l, d, at + layers * per + l] = 1.0
-        args.append(jnp.asarray(place, bf16))
-        outs = [jax.ShapeDtypeStruct((n * BLOCK, wide // 2), bf16)] * 2
+        outs = [jax.ShapeDtypeStruct((n * BLOCK, wide // PIECES), bf16)] * PIECES
+        place = [pltpu.VMEM((PIECES, layers, tall, n * BLOCK), bf16)]
     else:
         outs = [jax.ShapeDtypeStruct((layers, tall, wide), bf16)]
-    args += [jnp.asarray(perm, bf16), tok, cot, halo]
+        place = []
     outs += [jax.ShapeDtypeStruct((slots, d), bf16)] * 2 + [jax.ShapeDtypeStruct((slots, d), f32)] * 2
     vm = pl.BlockSpec(memory_space=pltpu.VMEM)
     return pl.pallas_call(
@@ -436,7 +450,8 @@
             pltpu.VMEM((rows, 3 * d), bf16),
             pltpu.VMEM((rows, d), bf16),
             pltpu.VMEM((layers, tall, wide), bf16),
-        ],
+            pltpu.VMEM((hidden_units, hidden_units), bf16),
+        ] + place,
         compiler_params=pltpu.CompilerParams(vmem_limit_bytes=vmem_bytes),
         name="two_layers",
     )(ranges, *args)
@@ -468,8 +483,7 @@
     slots, d = tokens.shape
     layers, part = vectors.shape
     flats = (attn_in, attn_out, mlp_in, mlp_out)
-    halo = jnp.concatenate([tokens, cotangent], axis=1)
-    fast = d % n == 0 and n & (n - 1) == 0 and layers * (d // n + 1) <= BLOCK and n >= 8
+    fast = d % n == 0 and n & (n - 1) == 0 and layers * (d // n + 1) <= BLOCK and n >= 32
     if fast:
         per = d // n
         block = rows_of(flats, d).reshape(layers * per, 12 * d)
@@ -477,12 +491,11 @@
         line = lax.dynamic_update_slice(line, vectors, (0, me * part))
         spare = jnp.zeros((BLOCK - layers * (per + 1), 12 * d), bf16)
         block = jnp.concatenate([block, line, spare], axis=0)
-        g_a, g_b, halo_in = gather(n, block[:, :6 * d], block[:, 6 * d:], halo)
-        s_a, s_b, act, act_up, dx, dx_up = compute(
-            n, True, ranges, (g_a, g_b), tokens, cotangent, halo_in, layers
+        *pieces, tok_up, cot_up = gather(n, block, tokens, cotangent)
+        *parts, act, act_up, dx, dx_up = compute(
+            n, True, ranges, pieces, tokens, cotangent, tok_up, cot_up, layers
         )
-        r_a, r_b, act, dx = scatter(n, s_a, s_b, act, act_up, dx, dx_up)
-        full = jnp.concatenate([r_a, r_b], axis=1)
+        full, act, dx = scatter(n, parts, act, act_up, dx, dx_up)
         grads = flats_of(full[:layers * per].reshape(layers, per, 12 * d), d)
         lines = full[layers * per:layers * (per + 1)]
         grads.append(lax.dynamic_slice(lines, (0, me * part), (layers, part)))
@@ -494,9 +507,10 @@
         line = whole.pop()
         spare = jnp.zeros((layers, BLOCK - 1, 12 * d), bf16)
         block = jnp.concatenate([rows_of(whole, d), line[:, None, :], spare], axis=1)
-        halo_in = lax.ppermute(halo, "dev", [(i, (i + n - 1) % n) for i in range(n)])
+        down = [(i, (i + n - 1) % n) for i in range(n)]
+        tok_up, cot_up = lax.ppermute(tokens, "dev", down), lax.ppermute(cotangent, "dev", down)
         grad, act, act_up, dx, dx_up = compute(
-            n, False, ranges, (block,), tokens, cotangent, halo_in, layers
+            n, False, ranges, (block,), tokens, cotangent, tok_up, cot_up, layers
         )
         up = [(i, (i + 1) % n) for i in range(n)]
         act = act + lax.ppermute(act_up, "dev", up)

time: 105 us -> 89.6 us (0.85)
  Pallas kernels: 87.7 us -> 76.3 us
  local copies, waits for them, and re-layouts: 15.7 us -> 11.4 us
    pallas_call x1, Pallas kernels: 33.7 us -> 27.8 us  [scatter(): pl.pallas_call(functools.partial(scatter_kernel, n), out_shape=(jax.Shape...]
    pallas_call x1, Pallas kernels: 31.4 us -> 25.8 us  [gather(): pl.pallas_call(functools.partial(gather_kernel, n), out_shape=(jax.ShapeD...]
    concatenate x5, local copies, waits for them, and re-layouts: 3.15 us -> 0.31 us  [rows_of(): jnp.concatenate([w_in.reshape(layers, -1, 3 * d), w_out.reshape(layers, -...]
    unnamed x15 -> x28, local copies, waits for them, and re-layouts: 8.06 us -> 8.88 us
where the time goes in v2:
time: 89.6 us; the launch traced here: 89.1 us
  Pallas kernels  76.3 us (85%)
  local copies, waits for them, and re-layouts  11.4 us (13%)
    pallas_call x1, Pallas kernels, scatter(): pl.pallas_call(functools.partial(scatter_kernel, n), out_shape=(jax.Shape...  27.8 us
    pallas_call x1, Pallas kernels, gather(): pl.pallas_call(functools.partial(gather_kernel, n), out_shape=(jax.ShapeD...  25.8 us
    pallas_call x1, Pallas kernels, compute(): pl.pallas_call(functools.partial(compute_kernel, n, fast, layers, d, hidd...  22.7 us
    unnamed x28, local copies, waits for them, and re-layouts  8.88 us

profile of v2, /device:TPU:0, one launch (start us, length us, event | category | flops | bytes accessed | tf_op | source)
XLA Modules:
  0.0 89.1 jit_solution(12547751239016134532)
XLA Ops:
  0.6 0.7 copy-done.7
  1.3 0.1 concatenate.16
  1.4 0.5 copy-done.9
  2.0 0.1 dynamic_update_slice.3
  2.1 0.7 copy.24.ranges
  2.8 0.1 concatenate.15
  2.9 0.6 copy-done.4
  3.5 0.7 copy-done.5
  4.2 0.1 concatenate.19
  4.3 0.7 pad_maximum_fusion.blk
  5.0 0.2 copy-done.2
  5.2 0.8 copy.22.tok.refs_6_
  6.0 0.1 copy-done.3
  6.1 0.8 copy.23.cot.refs_7_
  6.9 25.8 %gather_params.1 = (bf16[512,384]{1,0:T(8,128)(2,1)}, bf16[512,384]{1,0:T(8,128)(2,1)}, bf16[512,384]{1,0:T(8,128)(2,1)}, bf16[512,384]{1,0:T(8,128)(2,1)}, bf16...) custom-call(bf16[16,2304]{1,0:T(8,128)(2,1)} %pad_maximum_fusion.blk, ...), custom_call_target="tpu_custom_call" | custom-call | tf_op jit(solution)/shard_map/gather_params/pallas_call | solution.py:98
  32.7 22.7 %two_layers.1 = (bf16[512,384]{1,0:T(8,128)(2,1)}, bf16[512,384]{1,0:T(8,128)(2,1)}, bf16[512,384]{1,0:T(8,128)(2,1)}, bf16[512,384]{1,0:T(8,128)(2,1)}, bf16[51...) custom-call(s32[32,2]{1,0:T(8,128)} %copy.24.ranges, ...), custom_call_target="tpu_custom_call" | custom-call | tf_op jit(solution)/shard_map/two_layers/pallas_call | solution.py:431
  55.4 27.8 %scatter_grads.1 = (f32[16,2304]{1,0:T(8,128)}, bf16[256,192]{1,0:T(8,128)(2,1)}, f32[256,192]{1,0:T(8,128)}) custom-call(bf16[512,384]{1,0:T(8,128)(2,1)} %get-tuple-element.36.refs_0_, bf16[512,384]{1,0:T(8,128)(2,1)} %get-tuple-element.37.refs_1_, bf16[512,384]{1,0:T(8,128)(2,1)} %get-tuple-element.38.refs_2_, ...), custom_call_target="tpu_custom_call" | custom-call | tf_op jit(solution)/shard_map/scatter_grads/pallas_call | solution.py:193
  83.2 1.7 %copy.27 = bf16[256,192]{0,1:T(8,128)(2,1)} copy(bf16[256,192]{1,0:T(8,128)(2,1)} %get-tuple-element.56) | data formatting | bytes 196608
  84.9 0.6 constant_dynamic-slice_fusion
  85.7 0.7 reshape.44
  86.4 0.7 reshape.43
  87.1 0.6 copy.30
  87.7 0.6 copy.29
  88.3 0.8 copy.28
  (23 shorter events, 0.2 us)
Async XLA Ops:
  0.6 0.7 copy-start.7
  1.3 0.7 copy-start.9
  1.3 0.7 copy-start.8
  1.4 1.4 %copy-start.6 = (bf16[2,3456]{1,0:T(2,128)(2,1)S(1)}, bf16[2,3456]{1,0:T(2,128)(2,1)}, u32[]{:S(2)}) copy-start(bf16[2,3456]{1,0:T(2,128)(2,1)} %param.10) | copy-start | bytes 41476
  2.8 0.7 copy-start.4
  3.5 0.7 copy-start.5
  4.3 0.9 %copy-start.2 = (bf16[256,192]{0,1:T(8,128)(2,1)S(1)}, bf16[256,192]{0,1:T(8,128)(2,1)}, u32[]{:S(2)}) copy-start(bf16[256,192]{0,1:T(8,128)(2,1)} %param.8) | copy-start | bytes 294916
  5.2 0.9 %copy-start.3 = (bf16[256,192]{0,1:T(8,128)(2,1)S(1)}, bf16[256,192]{0,1:T(8,128)(2,1)}, u32[]{:S(2)}) copy-start(bf16[256,192]{0,1:T(8,128)(2,1)} %param.15) | copy-start | bytes 294916
  83.2 1.7 %copy-start.1 = (f32[16,2304]{1,0:T(8,128)S(1)}, f32[16,2304]{1,0:T(8,128)}, u32[]{:S(2)}) copy-start(f32[16,2304]{1,0:T(8,128)} %get-tuple-element.48) | copy-start | bytes 442372
  86.4 2.0 %copy-start = (f32[256,192]{1,0:T(8,128)S(1)}, f32[256,192]{1,0:T(8,128)}, u32[]{:S(2)}) copy-start(f32[256,192]{1,0:T(8,128)} %get-tuple-element.57) | copy-start | bytes 589828

commit v3 on v2

--- a/solution.py
+++ b/solution.py
@@ -99,7 +99,7 @@
         functools.partial(gather_kernel, n),
         out_shape=(jax.ShapeDtypeStruct((n * BLOCK, width), bf16),) * PIECES
         + (jax.ShapeDtypeStruct(tok.shape, bf16),) * 2,
-        in_specs=[vm] * 3,
+        in_specs=[vm] + [pl.BlockSpec(memory_space=pl.ANY)] * 2,
         out_specs=(vm,) * (PIECES + 2),
         scratch_shapes=[
             pltpu.SemaphoreType.DMA((PIECES, bits)),
@@ -178,7 +178,7 @@
     for copy in halo:
         copy.wait_recv()
     act_out[...] = act[...] + act_in[...]
-    dx_out[...] = dx[...] + dx_in[...]
+    dx_out[...] = dx[...] + dx_in[...].astype(f32)
     for copy in halo + list(copies.values()):
         copy.wait_send()
 
@@ -201,7 +201,7 @@
         out_specs=(vm,) * 3,
         scratch_shapes=boxes * (2 * PIECES) + totals * PIECES + [
             pltpu.VMEM(act.shape, act.dtype),
-            pltpu.VMEM(dx.shape, dx.dtype),
+            pltpu.VMEM(dx.shape, bf16),
             pltpu.SemaphoreType.DMA((PIECES, bits)),
             pltpu.SemaphoreType.DMA((PIECES, bits)),
             pltpu.SemaphoreType.DMA((2,)),
@@ -245,6 +245,14 @@
 
 def rows_sum(x):
     return jnp.sum(x, axis=0, keepdims=True)
+
+
+def goal_of(c, order, per, layers, l, d):
+    inside = c & (BLOCK - 1)
+    dev = sum(((c >> (4 + k)) & 1) << b for k, b in enumerate(order))
+    row = inside - l * per
+    goal = jnp.where((row >= 0) & (row < per), dev * per + row, -1)
+    return jnp.where(inside == layers * per + l, d, goal)
 
 
 def compute_kernel(n, fast, layers, width, hidden_units, ranges, *refs):
@@ -262,7 +270,7 @@
     act_own, act_up, dx_own, dx_up = take(4)
     w_all, w_one_s, w_two_s, hat1_s, h1_s, qkv_s, p_s, o_s, hat2_s, h2_s, slope_s, a_s = take(12)
     inv_s, dqkv_s, do_s, grad_s, perm = take(5)
-    slots = tok.shape[0]
+    slots = tok.shape[1]
     heads = width // HD
     d = width
     me = lax.axis_index("dev")
@@ -283,7 +291,7 @@
         picks.append(jnp.where(column == c, 1.0, 0.0).astype(bf16))
         valid_keys.append(lax.broadcasted_iota(jnp.int32, (ROWS, ROWS), 1) < count)
     pick = jnp.concatenate(picks, axis=0)
-    x = mm(pick[:, :slots], tok[...]) + mm(pick[:, slots:], tok_up[...])
+    x = mm_nt(pick[:, :slots], tok[...]) + mm_nt(pick[:, slots:], tok_up[...])
 
     unit = lax.broadcasted_iota(jnp.int32, (1, hidden_units), 1)
     group = sum(jnp.where(unit >= j * d, 1, 0) for j in range(1, 4))
@@ -291,19 +299,19 @@
     f = lax.broadcasted_iota(jnp.int32, (hidden_units, hidden_units), 0)
     perm[...] = jnp.where(f == origin, 1.0, 0.0).astype(bf16)
     if fast:
-        (place_s,) = take(1)
+        place_s, back_s = take(2)
         per = d // n
         orders = bit_orders(n)
         kinds = [orders[:c + 1].index(order) for c, order in enumerate(orders)]
         c = lax.broadcasted_iota(jnp.int32, (1, n * BLOCK), 1)
         line = lax.broadcasted_iota(jnp.int32, (d + BLOCK, n * BLOCK), 0)
-        inside = c & (BLOCK - 1)
-        for kind in set(kinds):
-            dev = sum(((c >> (4 + k)) & 1) << b for k, b in enumerate(orders[kind]))
+        c_down = lax.broadcasted_iota(jnp.int32, (n * BLOCK, 1), 0)
+        line_across = lax.broadcasted_iota(jnp.int32, (n * BLOCK, d + BLOCK), 1)
+        for kind in sorted(set(kinds)):
             for l in range(layers):
-                row = inside - l * per
-                goal = jnp.where((row >= 0) & (row < per), dev * per + row, -1)
-                goal = jnp.where(inside == layers * per + l, d, goal)
+                goal = goal_of(c_down, orders[kind], per, layers, l, d)
+                back_s[kind, l] = jnp.where(line_across == goal, 1.0, 0.0).astype(bf16)
+                goal = goal_of(c, orders[kind], per, layers, l, d)
                 place_s[kind, l] = jnp.where(line == goal, 1.0, 0.0).astype(bf16)
 
     vec = [None] * layers
@@ -354,10 +362,10 @@
         x = x1 + (mm(a_s[l], w_two_s[l]) + v_of(l, 7))
 
     x_low = x.astype(bf16)
-    act_own[...] = mm_tn(pick[:, :slots], x_low).astype(bf16)
-    act_up[...] = mm_tn(pick[:, slots:], x_low).astype(bf16)
-
-    dx = mm(pick[:, :slots], cot[...]) + mm(pick[:, slots:], cot_up[...])
+    act_own[...] = mm_tn(x_low, pick[:, :slots]).astype(bf16)
+    act_up[...] = mm_tn(x_low, pick[:, slots:]).astype(bf16)
+
+    dx = mm_nt(pick[:, :slots], cot[...]) + mm_nt(pick[:, slots:], cot_up[...])
     for l in reversed(range(layers)):
         dm = dx.astype(bf16)
         g_two = mm_tn(a_s[l], dm)
@@ -400,21 +408,21 @@
 
     high = dx.astype(bf16)
     low = (dx - high.astype(f32)).astype(bf16)
-    dx_own[...] = mm_tn(pick[:, :slots], high) + mm_tn(pick[:, :slots], low)
-    dx_up[...] = mm_tn(pick[:, slots:], high) + mm_tn(pick[:, slots:], low)
+    dx_own[...] = mm_tn(high, pick[:, :slots]) + mm_tn(low, pick[:, :slots])
+    dx_up[...] = mm_tn(high, pick[:, slots:]).astype(bf16)
     if fast:
         for c, out in enumerate(parts):
             cols = slice(c * out.shape[1], (c + 1) * out.shape[1])
-            part = mm_tn(place_s[kinds[c], 0], grad_s[0, :, cols])
+            part = mm(back_s[kinds[c], 0], grad_s[0, :, cols])
             for l in range(1, layers):
-                part += mm_tn(place_s[kinds[c], l], grad_s[l, :, cols])
+                part += mm(back_s[kinds[c], l], grad_s[l, :, cols])
             out[...] = part.astype(bf16)
     else:
         grad_out[...] = grad_s[...]
 
 
 def compute(n, fast, ranges, weights, tok, cot, tok_up, cot_up, layers):
-    slots, d = tok.shape
+    d, slots = tok.shape
     hidden_units = 4 * d
     rows = IMAGES_HERE * ROWS
     tall = d + BLOCK
@@ -422,11 +430,16 @@
     args = list(weights) + [tok, cot, tok_up, cot_up]
     if fast:
         outs = [jax.ShapeDtypeStruct((n * BLOCK, wide // PIECES), bf16)] * PIECES
-        place = [pltpu.VMEM((PIECES, layers, tall, n * BLOCK), bf16)]
+        place = [
+            pltpu.VMEM((PIECES, layers, tall, n * BLOCK), bf16),
+            pltpu.VMEM((PIECES, layers, n * BLOCK, tall), bf16),
+        ]
     else:
         outs = [jax.ShapeDtypeStruct((layers, tall, wide), bf16)]
         place = []
-    outs += [jax.ShapeDtypeStruct((slots, d), bf16)] * 2 + [jax.ShapeDtypeStruct((slots, d), f32)] * 2
+    outs += [
+        jax.ShapeDtypeStruct((d, slots), kind) for kind in (bf16, bf16, f32, bf16)
+    ]
     vm = pl.BlockSpec(memory_space=pltpu.VMEM)
     return pl.pallas_call(
         functools.partial(compute_kernel, n, fast, layers, d, hidden_units),
@@ -482,6 +495,7 @@
     me = lax.axis_index("dev")
     slots, d = tokens.shape
     layers, part = vectors.shape
+    tokens, cotangent = tokens.T, cotangent.T
     flats = (attn_in, attn_out, mlp_in, mlp_out)
     fast = d % n == 0 and n & (n - 1) == 0 and layers * (d // n + 1) <= BLOCK and n >= 32
     if fast:
@@ -523,7 +537,7 @@
             ])
             for term in terms
         ]
-    return (act, dx, *grads)
+    return (act.T, dx.T, *grads)
 
 
 def solution(mesh):

time: 89.6 us -> 85.3 us (0.952)
  Pallas kernels: 76.3 us -> 73.2 us
  local copies, waits for them, and re-layouts: 11.4 us -> 10.2 us
    unnamed x28 -> x22, local copies, waits for them, and re-layouts: 8.88 us -> 5.86 us
    pallas_call x1, Pallas kernels: 27.8 us -> 25 us  [scatter(): pl.pallas_call(functools.partial(scatter_kernel, n), out_shape=(jax.Shape...]
    reshape x1, local copies, waits for them, and re-layouts: 0.02 us -> 0.92 us  [local(): grads = flats_of(full[:layers * per].reshape(layers, per, 12 * d), d)]
where the time goes in v3:
time: 85.3 us; the launch traced here: 84.8 us
  Pallas kernels  73.2 us (86%)
  local copies, waits for them, and re-layouts  10.2 us (12%)
    pallas_call x1, Pallas kernels, gather(): pl.pallas_call(functools.partial(gather_kernel, n), out_shape=(jax.ShapeD...  25.6 us
    pallas_call x1, Pallas kernels, scatter(): pl.pallas_call(functools.partial(scatter_kernel, n), out_shape=(jax.Shape...  25 us
    pallas_call x1, Pallas kernels, compute(): pl.pallas_call(functools.partial(compute_kernel, n, fast, layers, d, hidd...  22.6 us
    unnamed x22, local copies, waits for them, and re-layouts  5.86 us

profile of v3, /device:TPU:0, one launch (start us, length us, event | category | flops | bytes accessed | tf_op | source)
XLA Modules:
  0.0 84.8 jit_solution(18176519619991838379)
XLA Ops:
  0.6 0.0 copy-start.5
  0.6 0.7 copy-done.5
  1.3 0.1 concatenate.16
  1.4 0.5 copy-done.7
  2.0 0.1 dynamic_update_slice.3
  2.1 0.7 copy.16.ranges
  2.8 0.1 concatenate.15
  2.9 0.6 copy-done.2
  3.5 0.7 copy-done.3
  4.2 0.1 concatenate.19
  4.3 0.7 pad_maximum_fusion.blk
  5.0 25.6 %gather_params.1 = (bf16[512,384]{1,0:T(8,128)(2,1)}, bf16[512,384]{1,0:T(8,128)(2,1)}, bf16[512,384]{1,0:T(8,128)(2,1)}, bf16[512,384]{1,0:T(8,128)(2,1)}, bf16...) custom-call(bf16[16,2304]{1,0:T(8,128)(2,1)} %pad_maximum_fusion.blk, ...), custom_call_target="tpu_custom_call" | custom-call | tf_op jit(solution)/shard_map/gather_params/pallas_call | solution.py:98
  30.6 22.6 %two_layers.1 = (bf16[512,384]{1,0:T(8,128)(2,1)}, bf16[512,384]{1,0:T(8,128)(2,1)}, bf16[512,384]{1,0:T(8,128)(2,1)}, bf16[512,384]{1,0:T(8,128)(2,1)}, bf16[51...) custom-call(s32[32,2]{1,0:T(8,128)} %copy.16.ranges, ...), custom_call_target="tpu_custom_call" | custom-call | tf_op jit(solution)/shard_map/two_layers/pallas_call | solution.py:444
  53.2 25.0 %scatter_grads.1 = (f32[16,2304]{1,0:T(8,128)}, bf16[192,256]{1,0:T(8,128)(2,1)}, f32[192,256]{1,0:T(8,128)}) custom-call(bf16[512,384]{1,0:T(8,128)(2,1)} %get-tuple-element.36.refs_0_, bf16[512,384]{1,0:T(8,128)(2,1)} %get-tuple-element.37.refs_1_, bf16[512,384]{1,0:T(8,128)(2,1)} %get-tuple-element.38.refs_2_, ...), custom_call_target="tpu_custom_call" | custom-call | tf_op jit(solution)/shard_map/scatter_grads/pallas_call | solution.py:193
  78.2 0.9 %slice.23 = f32[2,2304]{1,0:T(2,128)S(1)} slice(f32[16,2304]{1,0:T(8,128)} %get-tuple-element.48), slice={[12:14], [0:2304]} | slice | bytes 36864 | tf_op jit(solution)/shard_map/slice | solution.py:514
  79.1 0.6 constant_dynamic-slice_fusion
  79.8 0.9 %reshape.42 = f32[2,6,2304]{2,1,0:T(8,128)S(1)} reshape(f32[12,2304]{1,0:T(8,128)} %bitcast.16) | data formatting | bytes 221184 | tf_op jit(solution)/shard_map/reshape | solution.py:513
  80.7 0.1 slice.25
  80.8 0.7 reshape.44
  81.5 0.7 reshape.43
  82.2 0.6 copy.18
  82.8 0.6 copy.17
  83.5 0.6 copy.22
  84.1 0.7 copy.23
  (17 shorter events, 0.1 us)
Async XLA Ops:
  0.6 0.7 copy-start.5
  1.3 0.7 copy-start.7
  1.3 0.7 copy-start.6
  1.4 1.4 %copy-start.4 = (bf16[2,3456]{1,0:T(2,128)(2,1)S(1)}, bf16[2,3456]{1,0:T(2,128)(2,1)}, u32[]{:S(2)}) copy-start(bf16[2,3456]{1,0:T(2,128)(2,1)} %param.10) | copy-start | bytes 41476
  2.8 0.7 copy-start.2
  3.5 0.7 copy-start.3
  81.5 2.0 %copy-start.1 = (bf16[192,256]{1,0:T(8,128)(2,1)S(1)}, bf16[192,256]{1,0:T(8,128)(2,1)}, u32[]{:S(2)}) copy-start(bf16[192,256]{1,0:T(8,128)(2,1)} %get-tuple-element.46) | copy-start | bytes 294916
  82.2 1.9 %copy-start = (f32[192,256]{1,0:T(8,128)S(1)}, f32[192,256]{1,0:T(8,128)}, u32[]{:S(2)}) copy-start(f32[192,256]{1,0:T(8,128)} %get-tuple-element.47) | copy-start | bytes 589828
